TPU v7x, 512 devices: a whole 4x4x16 slice. The times are simulated.
512 devices in a mesh: row: 32 (over y_hi, z), col: 16 (over y_lo, x, core).
Axes of the slice: x: 4, y: 4 (y_hi: 2, y_lo: 2; y = y_hi * 2 + y_lo), z: 16, core: 2. Of those that a mesh axis runs over, the one named last changes fastest.
Arguments:
- pair_norm: bfloat16 [512, 512, 128], P('row', 'col'), may hold values from -6 to 6
- out_hat: bfloat16 [512, 512, 128], P('row', 'col'), may hold values from -4 to 4
- out_rstd: float32 [512, 512], P('row', 'col'), may hold values from 0.02 to 0.2
- grad_out: bfloat16 [512, 512, 128], P('row', 'col'), may hold values from -6 to 6
- token_mask: int32 [512], replicated, may hold values 0 or 1
- w_in: bfloat16 [128, 512], replicated, may hold values from -0.5 to 0.5
- w_gate: bfloat16 [128, 128], replicated, may hold values from -0.5 to 0.5
- w_out: bfloat16 [128, 128], replicated, may hold values from -0.5 to 0.5
- ln_gain: float32 [128], replicated, may hold values from 0.1 to 1.9
Outputs:
- d_pair: bfloat16 [512, 512, 128], P('row', 'col')
- d_win: float32 [128, 512], replicated
- d_wgate: float32 [128, 128], replicated
- d_wout: float32 [128, 128], replicated
- d_gain: float32 [128], replicated
All inputs are finite; a program needn't handle non-finite values.
Results may differ from a plain program's by a relative error of at most 0.0073.
Values may be sent and summed in bfloat16 or wider, within the bound.
A program may use at most 64 MiB of HBM per device.

v0:
```python
import jax
import jax.numpy as jnp
from jax import lax
from jax.sharding import PartitionSpec as P


def shards(pair_norm, out_hat, out_rstd, grad_out, token_mask, w_in, w_gate, w_out, ln_gain):
    tile_rows, tile_cols, width = pair_norm.shape
    token_count = token_mask.shape[0]
    pair_count = tile_rows * tile_cols
    row_index = lax.axis_index("row")
    col_index = lax.axis_index("col")
    mask_rows = lax.dynamic_slice_in_dim(token_mask, row_index * tile_rows, tile_rows).astype(
        jnp.float32
    )
    mask_cols = lax.dynamic_slice_in_dim(token_mask, col_index * tile_cols, tile_cols).astype(
        jnp.float32
    )
    pair_mask = (mask_rows[:, None] * mask_cols[None, :])[None]
    flat_pair = pair_norm.reshape(pair_count, width)
    projected = jnp.einsum("pc,cd->dp", flat_pair, w_in, preferred_element_type=jnp.float32)
    projected = projected.reshape(4 * width, tile_rows, tile_cols)
    value_a = projected[:width]
    logit_a = projected[width : 2 * width]
    value_b = projected[2 * width : 3 * width]
    logit_b = projected[3 * width :]
    sigma_a = jax.nn.sigmoid(logit_a)
    sigma_b = jax.nn.sigmoid(logit_b)
    left_cf = (pair_mask * sigma_a * value_a).astype(jnp.bfloat16)
    right_cf = (pair_mask * sigma_b * value_b).astype(jnp.bfloat16)
    left_slab, right_slab = (
        lax.all_to_all(left_cf, "col", split_axis=0, concat_axis=2, tiled=True),
        lax.all_to_all(right_cf, "col", split_axis=0, concat_axis=2, tiled=True),
    )
    gate = jax.nn.sigmoid(jnp.dot(flat_pair, w_gate, preferred_element_type=jnp.float32))
    normed = out_hat.reshape(pair_count, width).astype(jnp.float32)
    scaled = (normed * ln_gain).astype(jnp.bfloat16)
    output = jnp.dot(scaled, w_out, preferred_element_type=jnp.float32)
    grad_flat = grad_out.reshape(pair_count, width).astype(jnp.float32)
    gated_grad = (grad_flat * gate).astype(jnp.bfloat16)
    gate_grad = (grad_flat * output * gate * (1.0 - gate)).astype(jnp.bfloat16)
    part_wout = jnp.dot(scaled.T, gated_grad, preferred_element_type=jnp.float32)
    part_wgate = jnp.dot(flat_pair.T, gate_grad, preferred_element_type=jnp.float32)
    grad_scaled = jnp.einsum("pd,cd->pc", gated_grad, w_out, preferred_element_type=jnp.float32)
    part_gain = jnp.sum(grad_scaled * normed, axis=0)
    grad_normed = grad_scaled * ln_gain
    grad_mix = out_rstd.reshape(pair_count, 1) * (
        grad_normed
        - jnp.mean(grad_normed, axis=-1, keepdims=True)
        - normed * jnp.mean(grad_normed * normed, axis=-1, keepdims=True)
    )
    mix_cf = grad_mix.astype(jnp.bfloat16).T.reshape(width, tile_rows, tile_cols)
    mix_slab = lax.all_to_all(mix_cf, "col", split_axis=0, concat_axis=2, tiled=True)
    shard_rows = lax.all_gather(mix_slab, "row", axis=1, tiled=True)
    left_part = jnp.einsum(
        "ckj,cij->cki", right_slab, shard_rows, preferred_element_type=jnp.float32
    )
    right_total = jnp.einsum(
        "cki,cij->ckj", left_slab, shard_rows, preferred_element_type=jnp.float32
    )
    grad_left, grad_right = (
        lax.all_to_all(
            left_part.astype(jnp.bfloat16), "col", split_axis=2, concat_axis=0, tiled=True
        ),
        lax.all_to_all(
            right_total.astype(jnp.bfloat16), "col", split_axis=2, concat_axis=0, tiled=True
        ),
    )
    grad_left = grad_left.astype(jnp.float32)
    grad_right = grad_right.astype(jnp.float32)
    grad_proj = jnp.concatenate(
        [
            grad_left * pair_mask * sigma_a,
            grad_left * pair_mask * value_a * sigma_a * (1.0 - sigma_a),
            grad_right * pair_mask * sigma_b,
            grad_right * pair_mask * value_b * sigma_b * (1.0 - sigma_b),
        ],
        axis=0,
    ).astype(jnp.bfloat16)
    grad_proj = grad_proj.reshape(4 * width, pair_count)
    part_win = jnp.einsum("pc,dp->cd", flat_pair, grad_proj, preferred_element_type=jnp.float32)
    d_pair = jnp.einsum(
        "dp,cd->pc", grad_proj, w_in, preferred_element_type=jnp.float32
    ) + jnp.einsum("pd,cd->pc", gate_grad, w_gate, preferred_element_type=jnp.float32)
    d_pair = d_pair.astype(jnp.bfloat16).reshape(tile_rows, tile_cols, width)
    total_win, total_wgate, total_wout, total_gain = lax.psum(
        (part_win, part_wgate, part_wout, part_gain), ("row", "col")
    )
    return (
        d_pair,
        total_win / token_count,
        total_wgate / token_count,
        total_wout / token_count,
        total_gain / token_count,
    )


def solution(mesh):
    in_specs = (
        P("row", "col", None),
        P("row", "col", None),
        P("row", "col"),
        P("row", "col", None),
        P(),
        P(),
        P(),
        P(),
        P(),
    )
    out_specs = (P("row", "col", None), P(), P(), P(), P())
    return jax.shard_map(shards, mesh=mesh, in_specs=in_specs, out_specs=out_specs, check_vma=False)
```

profile of v0, /device:TPU:1, one launch (start us, length us, event | category | flops | bytes accessed | tf_op | source)
XLA Modules:
  0.0 723.6 jit_solution(9327776645122602594)
XLA Ops:
  7.2 0.8 mul.183
  8.1 1.1 fusion.22
  9.2 1.3 fusion.28
  10.5 1.2 fusion.27
  11.7 0.4 copy.41
  12.2 0.5 reshape.128
  12.7 15.6 %all_to_all.72 = bf16[16,2,2048]{2,1,0:T(2,128)(2,1)S(1)} all-to-all(bf16[16,2,2048]{2,1,0:T(2,128)(2,1)S(1)} %reshape.128), channel_id=1, replica_groups=mesh['row'=32,'col'=16] {'col'}, dimensions={0} | all-to-all | bytes 262144 | tf_op jit(solution)/shard_map/all_to_all | solution.py:53
  28.3 0.3 reshape.129
  28.5 0.3 copy.42
  28.9 1.1 all_to_all.60
  30.3 0.3 fusion.38
  30.6 0.9 fusion.34
  31.5 0.7 copy-done.1
  32.3 0.4 copy.39
  32.8 1.2 reshape.132
  33.9 3.8 all-to-all-start
  37.8 110.1 %psum.31 = f32[128]{0:T(128)S(1)} all-reduce(f32[128]{0:T(128)S(1)} %get-tuple-element.20), channel_id=1, replica_groups=mesh['row'=32,'col'=16] {'row','col'}, use_global_device_ids=true, to_apply=%region_6.0 | all-reduce | flops 128 | bytes 1024 | tf_op jit(solution)/shard_map/psum | solution.py:86
  147.9 0.9 fusion.5
  148.8 0.3 reshape.133
  149.0 0.3 copy.40
  149.4 0.4 all_to_all.56
  149.9 36.8 %all-gather.2.cloned.1.call-done = bf16[8,512,512]{2,1,0:T(8,128)(2,1)} async-done(((bf16[8,16,512]{2,1,0:T(8,128)(2,1)}), bf16[8,512,512]{2,1,0:T(8,128)(2,1)}) %all-gather.2.cloned.1.call-update) | async-done | bytes 4194320 | tf_op jit(solution)/shard_map/all_gather | solution.py:54
  186.6 3.4 convolution_convert_fusion.1
  190.0 0.8 copy.43
  190.8 1.8 reshape.134
  192.6 13.1 %all-to-all-start.2 = ((bf16[16,2,2048]{2,1,0:T(2,128)(2,1)}), bf16[16,2,2048]{2,1,0:T(2,128)(2,1)S(1)}, u32[]{:S(2)}, u32[]{:S(2)}) async-start(bf16[16,2,2048]{2,1,0:T(2,128)(2,1)} %reshape.134), calls=%async_computation.2 | async-start | bytes 262144 | tf_op jit(solution)/shard_map/all_to_all | solution.py:62
  205.6 0.9 fusion.37
  206.5 5.2 all-to-all-done.2
  211.7 0.7 reshape.135
  212.4 0.6 copy.44
  213.0 0.4 copy.51
  213.4 1.9 multiply_convert_fusion.3
  215.4 0.4 copy.46
  215.8 1.2 reshape.126
  217.0 3.8 all-to-all-start.3
  220.8 1.8 convolution_bitcast_fusion.1
  222.5 4.4 all-to-all-done.3
  226.9 0.3 reshape.127
  227.2 0.3 copy.47
  227.5 0.4 all_to_all.65
  228.0 3.5 convolution_convert_fusion
  231.5 1.7 copy.48
  233.2 1.8 reshape.130
  234.9 4.4 all-to-all-start.4
  239.3 0.5 broadcast_multiply_fusion.6
  239.9 0.4 reshape.117
  240.3 0.8 copy.45
  241.1 4.4 all-to-all-done.4
  245.6 1.9 reshape.131
  247.4 0.6 copy.49
  248.1 0.4 reshape.118
  248.6 0.4 copy.52
  249.1 1.1 multiply_convert_fusion.1
  250.2 0.3 multiply_convert_fusion.8
  250.5 1.9 convolution_bitcast_fusion
  252.5 0.3 fusion.7
  252.8 0.8 fusion.6
  253.6 458.2 %all-reduce.3.cloned.1.call-done = (f32[128,512]{0,1:T(8,128)}, f32[128,128]{0,1:T(8,128)}, f32[128,128]{0,1:T(8,128)}) async-done(((f32[128,512]{0,1:T(8,128)}, f32[128,128]{0,1:T(8,128)}, f32[128,128]{0,1:T(8,128)}), (f32[128,512]{0,1:T(8,128)}, f32[128,128]{0,1:T(8,128)}, f32[128,128]{0,1:T(8,128)})) %all-reduce.3.cloned.1.call-update) | async-done | bytes 393232 | tf_op jit(solution)/shard_map/psum | solution.py:86
  711.8 1.0 broadcast_multiply_fusion
  712.8 0.8 copy.54
  713.6 0.8 broadcast_multiply_fusion.2
  714.5 0.7 copy.55
  715.2 0.8 broadcast_multiply_fusion.1
  716.1 0.7 copy.56
  (33 shorter events, 0.7 us)
Async XLA Ops:
  7.2 0.9 copy-start
  7.2 22.9 %copy-start.10 = (s32[512]{0:T(512)S(1)}, s32[512]{0:T(512)}, u32[]{:S(2)}) copy-start(s32[512]{0:T(512)} %param.13) | copy-start | bytes 6148
  7.2 23.1 %copy-start.4 = (bf16[128,512]{1,0:T(8,128)(2,1)S(1)}, bf16[128,512]{1,0:T(8,128)(2,1)}, u32[]{:S(2)}) copy-start(bf16[128,512]{1,0:T(8,128)(2,1)} %param.14) | copy-start | bytes 393220
  7.2 179.4 %all-gather.2.cloned.1.call-start = ((), (), s32[]{:S(2)}) async-start(), calls=%async_computation.5 | async-start | bytes 4325376 | tf_op jit(solution)/shard_map/all_gather | solution.py:54
  12.7 135.2 %copy-start.7 = (bf16[16,32,128]{2,1,0:T(8,128)(2,1)S(1)}, bf16[16,32,128]{2,1,0:T(8,128)(2,1)}, u32[]{:S(2)}) copy-start(bf16[16,32,128]{2,1,0:T(8,128)(2,1)} %param.12) | copy-start | bytes 393220
  12.7 135.2 %copy-start.8 = (bf16[128,128]{1,0:T(8,128)(2,1)S(1)}, bf16[128,128]{1,0:T(8,128)(2,1)}, u32[]{:S(2)}) copy-start(bf16[128,128]{1,0:T(8,128)(2,1)} %param.16) | copy-start | bytes 98308
  31.5 0.7 copy-start.1
  33.9 114.8 %all-to-all-start = ((bf16[16,2,2048]{2,1,0:T(2,128)(2,1)}), bf16[16,2,2048]{2,1,0:T(2,128)(2,1)S(1)}, u32[]{:S(2)}, u32[]{:S(2)}) async-start(bf16[16,2,2048]{2,1,0:T(2,128)(2,1)} %reshape.132), calls=%async_computation | async-start | bytes 262144 | tf_op jit(solution)/shard_map/all_to_all | solution.py:33
  192.6 19.2 %all-to-all-start.2 = ((bf16[16,2,2048]{2,1,0:T(2,128)(2,1)}), bf16[16,2,2048]{2,1,0:T(2,128)(2,1)S(1)}, u32[]{:S(2)}, u32[]{:S(2)}) async-start(bf16[16,2,2048]{2,1,0:T(2,128)(2,1)} %reshape.134), calls=%async_computation.2 | async-start | bytes 262144 | tf_op jit(solution)/shard_map/all_to_all | solution.py:62
  217.0 9.9 %all-to-all-start.3 = ((bf16[16,2,2048]{2,1,0:T(2,128)(2,1)}), bf16[16,2,2048]{2,1,0:T(2,128)(2,1)S(1)}, u32[]{:S(2)}, u32[]{:S(2)}) async-start(bf16[16,2,2048]{2,1,0:T(2,128)(2,1)} %reshape.126), calls=%async_computation.3 | async-start | bytes 262144 | tf_op jit(solution)/shard_map/all_to_all | solution.py:32
  234.9 10.6 %all-to-all-start.4 = ((bf16[16,2,2048]{2,1,0:T(2,128)(2,1)}), bf16[16,2,2048]{2,1,0:T(2,128)(2,1)}, u32[]{:S(2)}, u32[]{:S(2)}) async-start(bf16[16,2,2048]{2,1,0:T(2,128)(2,1)} %reshape.130), calls=%async_computation.4 | async-start | bytes 262144 | tf_op jit(solution)/shard_map/all_to_all | solution.py:65
  239.3 472.5 %all-reduce.3.cloned.1.call-start = ((), (), s32[]{:S(2)}) async-start(), calls=%async_computation.6 | async-start | bytes 786432 | tf_op jit(solution)/shard_map/psum | solution.py:86
  248.1 2.2 copy-start.3
  248.1 2.4 copy-start.6
  248.5 4.0 copy-start.5
  249.0 3.7 copy-start.2
  249.1 3.7 copy-start.9
Sparse Core Ops, SparseCore 0:
  30.2 156.4 all-gather.1
  252.6 459.2 all-reduce.2
where the time goes:
time: 725 us; the launch traced here: 724 us
  waiting for transfers between devices  509 us (70%)
  blocking collectives  126 us (17%)
  starting transfers between devices  25.1 us (3%)
  local copies, waits for them, and re-layouts  24.4 us (3%)
  matrix products  16.2 us (2%)
  between operations  14.4 us (2%)
  other arithmetic  8.89 us (1%)
    psum x1, waiting for transfers between devices, shards(): lax.psum((part_win, part_wgate, part_wout, part_gain), ('row', 'col'))  458 us
    psum x1, blocking collectives, shards(): lax.psum((part_win, part_wgate, part_wout, part_gain), ('row', 'col'))  110 us
    all_gather x1, waiting for transfers between devices, shards(): shard_rows = lax.all_gather(mix_slab, 'row', axis=1, tiled=True)  36.8 us
    all_to_all x1, blocking collectives, shards(): lax.all_to_all(mix_cf, 'col', split_axis=0, concat_axis=2, tiled=True)  15.6 us
  transfers between devices with their start and end apart: 6, of which 5 were waited for; matrix products, arithmetic and copies ran while one was open for 1% of the time, Pallas kernels for 0%

commit v1 on v0

v1 whole, which is shorter than its diff:
```python
import jax
import jax.numpy as jnp
from jax import lax
from jax.experimental import pallas as pl
from jax.experimental.pallas import tpu as pltpu
from jax.sharding import PartitionSpec as P

F32, BF16 = jnp.float32, jnp.bfloat16
MESH = pl.DeviceIdType.MESH

TOKENS = 512
WIDTH = 128
ROWS, COLS = 16, 32
PAIRS = ROWS * COLS
RING = 16
BANKS = 2
ACROSS = 16
PLANE = BANKS * ACROSS
SLOTS = WIDTH // PLANE
CHUNK = 128 // SLOTS


def mm(a, b, ca, cb):
    return lax.dot_general(a, b, (((ca,), (cb,)), ((), ())), preferred_element_type=F32)


def swap_chunks(parts):
    lane = lax.broadcasted_iota(jnp.int32, parts[0].shape, 1)
    low = lane < 64
    even = lax.rem(lane // CHUNK, 2) == 0
    a, b, c, d = parts
    a, c = jnp.where(low, a, pltpu.roll(c, 64, 1)), jnp.where(low, pltpu.roll(a, 64, 1), c)
    b, d = jnp.where(low, b, pltpu.roll(d, 64, 1)), jnp.where(low, pltpu.roll(b, 64, 1), d)
    a, b = jnp.where(even, a, pltpu.roll(b, 32, 1)), jnp.where(even, pltpu.roll(a, 96, 1), b)
    c, d = jnp.where(even, c, pltpu.roll(d, 32, 1)), jnp.where(even, pltpu.roll(c, 96, 1), d)
    return a, b, c, d


def to_tiles(values, work):
    parts = []
    for slot in range(SLOTS):
        block = values[slot * PLANE : (slot + 1) * PLANE]
        parts.append(jnp.concatenate([block[:, g * 128 : (g + 1) * 128] for g in range(4)], axis=0))
    for low, part in enumerate(swap_chunks(parts)):
        for g in range(4):
            work[pl.ds(4 * g + low, PLANE, stride=ROWS), :] = part[g * PLANE : (g + 1) * PLANE]
    return work[...].astype(BF16).reshape(PLANE, ROWS, 128)


def from_tiles(tiles, work):
    work[...] = tiles.astype(F32).reshape(PLANE * ROWS, 128)
    parts = []
    for low in range(4):
        parts.append(
            jnp.concatenate(
                [work[pl.ds(4 * g + low, PLANE, stride=ROWS), :] for g in range(4)], axis=0
            )
        )
    out = []
    for part in swap_chunks(parts):
        out.append(
            jnp.concatenate([part[g * PLANE : (g + 1) * PLANE] for g in range(4)], axis=1)
        )
    return jnp.concatenate(out, axis=0)


def gather_slab(tiles):
    tiles = tiles.astype(F32).reshape(BANKS, 4, 4, ROWS, 128)
    parts = [tiles[:, :, q].reshape(BANKS * 4 * ROWS, 128) for q in range(4)]
    out = []
    for part in swap_chunks(parts):
        part = part.reshape(BANKS, 4, ROWS, 128)
        out.append(
            jnp.concatenate([part[:, g].reshape(BANKS * ROWS, 128) for g in range(4)], axis=1)
        )
    return jnp.concatenate(out, axis=0)


def scatter_slab(slab):
    parts = []
    for slot in range(SLOTS):
        block = slab[slot * BANKS * ROWS : (slot + 1) * BANKS * ROWS]
        block = [
            block[:, g * 128 : (g + 1) * 128].reshape(BANKS, 1, ROWS, 128) for g in range(4)
        ]
        parts.append(jnp.concatenate(block, axis=1).reshape(BANKS * 4 * ROWS, 128))
    out = [
        part.reshape(BANKS, 4, 1, ROWS, 128) for part in swap_chunks(parts)
    ]
    return jnp.concatenate(out, axis=2).reshape(PLANE, ROWS, 128).astype(BF16)


def kernel(
    pair_ref, hat_ref, rstd_ref, grad_ref, mask_ref, win_ref, wgate_ref, wout_ref, gain_ref,
    dpair_ref, dwin_ref, dwgate_ref, dwout_ref, dgain_ref,
    work, mix_out, mix_in, lr_out, lr_in, back_out, back_in,
    held, right_diag, left_cols, left_sums, right_sums, factors, proj,
    small_out, small_in, small_sum, small_row, small_mine, small_part, small_all,
    win_out, win_in, win_sum, win_row, win_mine, win_part, win_all,
    ring_send, ring_recv, send_sems, recv_sems,
):
    row, col = lax.axis_index("row"), lax.axis_index("col")
    bank, z = row // RING, lax.rem(row, RING)
    me = bank * ACROSS + col

    def plane_id(peer):
        return ((peer // ACROSS) * RING + z, lax.rem(peer, ACROSS))

    def ring_id(place):
        return (bank * RING + place, col)

    barrier = pltpu.get_barrier_semaphore()

    @pl.loop(1, PLANE)
    def _(t):
        pl.semaphore_signal(
            barrier, inc=1, device_id=plane_id(lax.rem(me + t, PLANE)), device_id_type=MESH
        )

    @pl.loop(1, RING)
    def _(t):
        pl.semaphore_signal(
            barrier, inc=1, device_id=ring_id(lax.rem(z + t, RING)), device_id_type=MESH
        )

    def plane_send(source, target, k):
        @pl.loop(1, PLANE)
        def _(t):
            peer = lax.rem(me + t, PLANE)
            pltpu.make_async_remote_copy(
                src_ref=source(peer), dst_ref=target.at[me],
                send_sem=send_sems.at[k], recv_sem=recv_sems.at[k],
                device_id=plane_id(peer), device_id_type=MESH,
            ).start()

    def ring_send_rows(source, target, k):
        @pl.loop(1, RING)
        def _(t):
            peer = lax.rem(z + t, RING)
            pltpu.make_async_remote_copy(
                src_ref=source(peer), dst_ref=target.at[pl.ds(z, 1)],
                send_sem=send_sems.at[k], recv_sem=recv_sems.at[k],
                device_id=ring_id(peer), device_id_type=MESH,
            ).start()

    def wait_bytes(ref, sem):
        pltpu.make_async_copy(ref, ref, sem).wait()

    def wait_many(target, count, k):
        wait_bytes(target.at[pl.ds(0, count - 1)], recv_sems.at[k])

    def hop(way, s, part):
        step = 1 if way == 0 else RING - 1
        block = lax.rem(z + (RING - 1) * step * (s - 1), RING)
        return pltpu.make_async_remote_copy(
            src_ref=held.at[block, part], dst_ref=held.at[block, part],
            send_sem=ring_send.at[way, s - 1, part], recv_sem=ring_recv.at[way, s - 1, part],
            device_id=ring_id(lax.rem(z + step, RING)), device_id_type=MESH,
        )

    x = pair_ref[...].reshape(PAIRS, WIDTH)
    hat = hat_ref[...].reshape(PAIRS, WIDTH).astype(F32).T
    grad = grad_ref[...].reshape(PAIRS, WIDTH).astype(F32).T
    diagonal = lax.broadcasted_iota(jnp.int32, (WIDTH, WIDTH), 0) == lax.broadcasted_iota(
        jnp.int32, (WIDTH, WIDTH), 1
    )
    gain = jnp.sum(jnp.where(diagonal, gain_ref[...], 0.0), axis=1, keepdims=True)
    pair_mask = mask_ref[...]
    gate = jax.nn.sigmoid(mm(wgate_ref[...], x, 0, 1))
    gated = (grad * gate).astype(BF16)
    scaled_grad = mm(wout_ref[...], gated, 1, 0)
    h = scaled_grad * gain
    mean_h = jnp.mean(h, axis=0, keepdims=True)
    mean_hx = jnp.mean(h * hat, axis=0, keepdims=True)
    mix = rstd_ref[...] * (h - mean_h - hat * mean_hx)
    mix_out[...] = to_tiles(mix, work)
    mix_in[me] = mix_out[me]
    pl.semaphore_wait(barrier, PLANE + RING - 2)
    plane_send(lambda peer: mix_out.at[peer], mix_in, 0)

    projected = mm(win_ref[...], x, 0, 1)
    value_a, logit_a = projected[:WIDTH], projected[WIDTH : 2 * WIDTH]
    value_b, logit_b = projected[2 * WIDTH : 3 * WIDTH], projected[3 * WIDTH :]
    sigma_a, sigma_b = jax.nn.sigmoid(logit_a), jax.nn.sigmoid(logit_b)
    masked_a, masked_b = pair_mask * sigma_a, pair_mask * sigma_b
    lr_out[:, :ROWS] = to_tiles(masked_a * value_a, work)
    lr_out[:, ROWS:] = to_tiles(masked_b * value_b, work)
    lr_in[me] = lr_out[me]
    plane_send(lambda peer: lr_out.at[peer], lr_in, 1)
    factors[0] = masked_a
    factors[1] = masked_a * value_a * (1.0 - sigma_a)
    factors[2] = masked_b
    factors[3] = masked_b * value_b * (1.0 - sigma_b)

    wait_many(mix_in, PLANE, 0)
    slab = gather_slab(mix_in[...]).astype(BF16)
    for slot in range(SLOTS):
        held[z, slot // 2, :, (slot % 2) * TOKENS : (slot % 2 + 1) * TOKENS] = slab[
            slot * BANKS * ROWS : (slot + 1) * BANKS * ROWS
        ]
    for part in range(2):
        for way in range(2):
            hop(way, 1, part).start()

    scaled = (hat * gain).astype(BF16)
    output = mm(wout_ref[...], scaled, 0, 0)
    gate_grad = (grad * output * gate * (1.0 - gate)).astype(BF16)
    proj[4 * WIDTH :] = gate_grad
    small_out[: PLANE // 2, :8] = mm(x, gate_grad, 0, 1).reshape(PLANE // 2, 8, WIDTH)
    small_out[PLANE // 2 :, :8] = mm(scaled, gated, 1, 1).reshape(PLANE // 2, 8, WIDTH)
    part_gain = jnp.sum(scaled_grad * hat, axis=1, keepdims=True)
    part_gain = jnp.sum(jnp.where(diagonal, part_gain, 0.0), axis=0, keepdims=True)
    small_out[:, 8:] = jnp.broadcast_to(part_gain[None], (PLANE, 8, WIDTH))
    small_in[me] = small_out[me]
    plane_send(lambda peer: small_out.at[peer], small_in, 2)

    wait_many(lr_in, PLANE, 1)
    left_cols[...] = gather_slab(lr_in[:, :ROWS]).T.astype(BF16)
    right = gather_slab(lr_in[:, ROWS:]).astype(BF16)
    right_diag[...] = jnp.zeros_like(right_diag)
    for slot in range(SLOTS):
        rows = slice(slot * BANKS * ROWS, (slot + 1) * BANKS * ROWS)
        right_diag[slot // 2, rows, (slot % 2) * TOKENS : (slot % 2 + 1) * TOKENS] = right[rows]
    right_sums[...] = jnp.zeros_like(right_sums)

    def contract(part, blocks):
        mixes = jnp.concatenate([held[block, part] for block in blocks], axis=0)
        places = [
            pl.ds(pl.multiple_of(b * (TOKENS // BANKS) + block * ROWS, ROWS), ROWS)
            for block in blocks
            for b in range(BANKS)
        ]
        sums = mm(mixes, right_diag[part], 1, 1)
        for n, place in enumerate(places):
            piece = sums[n * ROWS : (n + 1) * ROWS]
            if part:
                piece = piece + left_sums[place]
            left_sums[place] = piece
        lefts = jnp.concatenate([left_cols[place] for place in places], axis=0)
        for c in range(2):
            rows = slice((2 * part + c) * BANKS * ROWS, (2 * part + c + 1) * BANKS * ROWS)
            right_sums[rows] += mm(
                lefts[:, rows], mixes[:, c * TOKENS : (c + 1) * TOKENS], 0, 0
            )

    contract(0, [z])
    contract(1, [z])

    def ring_step(s, last):
        for part in range(2):
            for way in range(2):
                hop(way, s, part).wait_recv()
                if not last or way == part:
                    hop(way, s + 1, part).start()
            contract(part, [lax.rem(z + RING - s, RING), lax.rem(z + s, RING)])

    def close(total, row_in, mine, part, full, k):
        row_in[pl.ds(z, 1)] = total[pl.ds(z, 1)]
        ring_send_rows(lambda peer: total.at[pl.ds(peer, 1)], row_in, k)

    ring_step(1, False)
    ring_step(2, False)
    wait_many(small_in, PLANE, 2)
    small_sum[...] = jnp.sum(small_in[...], axis=0)
    small_row[pl.ds(z, 1)] = small_sum[pl.ds(z, 1)]
    ring_send_rows(lambda peer: small_sum.at[pl.ds(peer, 1)], small_row, 3)
    ring_step(3, False)
    ring_step(4, False)
    wait_many(small_row, RING, 3)
    small_mine[...] = jnp.sum(small_row[...], axis=0, keepdims=True) * (1.0 / TOKENS)
    small_part[pl.ds(z, 1)] = small_mine[...]
    ring_send_rows(lambda peer: small_mine, small_part, 4)
    ring_step(5, False)
    ring_step(6, False)
    wait_many(small_part, RING, 4)
    small_all[me] = small_part[:8]
    plane_send(lambda peer: small_part.at[pl.ds(0, 8)], small_all, 5)
    ring_step(7, True)
    for part in range(2):
        hop(part, RING // 2, part).wait_recv()
        contract(part, [lax.rem(z + RING // 2, RING)])

    back_out[:, :ROWS] = scatter_slab(left_sums[...].T)
    back_out[:, ROWS:] = scatter_slab(right_sums[...])
    back_in[me] = back_out[me]
    plane_send(lambda peer: back_out.at[peer], back_in, 6)
    wait_many(small_all, PLANE, 5)
    dwgate_ref[...] = small_all[: PLANE // 2].reshape(WIDTH, WIDTH)
    dwout_ref[...] = small_all[PLANE // 2 :].reshape(WIDTH, WIDTH)
    dgain_ref[...] = small_part[8:9]

    wait_many(back_in, PLANE, 6)
    grad_left = from_tiles(back_in[:, :ROWS], work)
    proj[:WIDTH] = (grad_left * factors[0]).astype(BF16)
    proj[WIDTH : 2 * WIDTH] = (grad_left * factors[1]).astype(BF16)
    grad_right = from_tiles(back_in[:, ROWS:], work)
    proj[2 * WIDTH : 3 * WIDTH] = (grad_right * factors[2]).astype(BF16)
    proj[3 * WIDTH : 4 * WIDTH] = (grad_right * factors[3]).astype(BF16)

    win_out[...] = mm(proj[: 4 * WIDTH], x, 1, 0).reshape(PLANE, ROWS, WIDTH)
    win_in[me] = win_out[me]
    plane_send(lambda peer: win_out.at[peer], win_in, 7)
    weights = jnp.concatenate([win_ref[...], wgate_ref[...]], axis=1)
    d_pair = mm(weights, proj[...], 1, 0)
    dpair_ref[...] = d_pair.T.astype(BF16).reshape(ROWS, COLS, WIDTH)
    wait_many(win_in, PLANE, 7)
    win_sum[...] = jnp.sum(win_in[...], axis=0)
    win_row[pl.ds(z, 1)] = win_sum[pl.ds(z, 1)]
    ring_send_rows(lambda peer: win_sum.at[pl.ds(peer, 1)], win_row, 8)
    wait_many(win_row, RING, 8)
    win_mine[...] = jnp.sum(win_row[...], axis=0, keepdims=True) * (1.0 / TOKENS)
    win_part[pl.ds(z, 1)] = win_mine[...]
    ring_send_rows(lambda peer: win_mine, win_part, 9)
    wait_many(win_part, RING, 9)
    win_all[me] = win_part[...]
    plane_send(lambda peer: win_part, win_all, 10)
    wait_many(win_all, PLANE, 10)
    dwin_ref[...] = win_all[...].reshape(4 * WIDTH, WIDTH).T

    for k, ref in enumerate(
        [mix_in, lr_in, small_in, None, None, small_all, back_in, win_in, None, None, win_all]
    ):
        if ref is None:
            wait_bytes(win_row.at[pl.ds(0, RING - 1)], send_sems.at[k])
        else:
            wait_bytes(ref.at[pl.ds(0, PLANE - 1)], send_sems.at[k])
    for s in range(1, RING // 2 + 1):
        for part in range(2):
            for way in range(2):
                if s < RING // 2 or way == part:
                    hop(way, s, part).wait_send()


def shards(pair_norm, out_hat, out_rstd, grad_out, token_mask, w_in, w_gate, w_out, ln_gain):
    row, col = lax.axis_index("row"), lax.axis_index("col")
    mask = token_mask.astype(F32)
    mask_rows = lax.dynamic_slice_in_dim(mask, row * ROWS, ROWS)
    mask_cols = lax.dynamic_slice_in_dim(mask, col * COLS, COLS)
    pair_mask = (mask_rows[:, None] * mask_cols[None, :]).reshape(1, PAIRS)
    tile = (ROWS, COLS, WIDTH)
    vmem = pl.BlockSpec(memory_space=pltpu.VMEM)
    reduction = lambda rows: [
        pltpu.VMEM((PLANE, ROWS, WIDTH), F32),
        pltpu.VMEM((PLANE, ROWS, WIDTH), F32),
        pltpu.VMEM((RING, WIDTH), F32),
        pltpu.VMEM((RING, WIDTH), F32),
        pltpu.VMEM((1, WIDTH), F32),
        pltpu.VMEM((RING, WIDTH), F32),
        pltpu.VMEM((PLANE, rows, WIDTH), F32),
    ]
    d_pair, d_win, d_wgate, d_wout, d_gain = pl.pallas_call(
        kernel,
        out_shape=(
            jax.ShapeDtypeStruct(tile, BF16),
            jax.ShapeDtypeStruct((WIDTH, 4 * WIDTH), F32),
            jax.ShapeDtypeStruct((WIDTH, WIDTH), F32),
            jax.ShapeDtypeStruct((WIDTH, WIDTH), F32),
            jax.ShapeDtypeStruct((1, WIDTH), F32),
        ),
        in_specs=[vmem] * 9,
        out_specs=[vmem] * 5,
        scratch_shapes=[
            pltpu.VMEM((PAIRS, WIDTH), F32),
            pltpu.VMEM((PLANE, ROWS, WIDTH), BF16),
            pltpu.VMEM((PLANE, ROWS, WIDTH), BF16),
            pltpu.VMEM((PLANE, 2 * ROWS, WIDTH), BF16),
            pltpu.VMEM((PLANE, 2 * ROWS, WIDTH), BF16),
            pltpu.VMEM((PLANE, 2 * ROWS, WIDTH), BF16),
            pltpu.VMEM((PLANE, 2 * ROWS, WIDTH), BF16),
            pltpu.VMEM((RING, 2, BANKS * ROWS, 2 * TOKENS), BF16),
            pltpu.VMEM((2, WIDTH, 2 * TOKENS), BF16),
            pltpu.VMEM((TOKENS, WIDTH), BF16),
            pltpu.VMEM((TOKENS, WIDTH), F32),
            pltpu.VMEM((WIDTH, TOKENS), F32),
            pltpu.VMEM((4, WIDTH, PAIRS), F32),
            pltpu.VMEM((5 * WIDTH, PAIRS), BF16),
            *reduction(8),
            *reduction(ROWS),
            pltpu.SemaphoreType.DMA((2, RING // 2, 2)),
            pltpu.SemaphoreType.DMA((2, RING // 2, 2)),
            pltpu.SemaphoreType.DMA((11,)),
            pltpu.SemaphoreType.DMA((11,)),
        ],
        compiler_params=pltpu.CompilerParams(
            collective_id=0, has_side_effects=True, vmem_limit_bytes=40 * 1024 * 1024
        ),
    )(
        pair_norm, out_hat, out_rstd.reshape(1, PAIRS), grad_out, pair_mask,
        w_in, w_gate, w_out, ln_gain.reshape(1, WIDTH),
    )
    return d_pair, d_win, d_wgate, d_wout, d_gain.reshape(WIDTH)


def solution(mesh):
    tile = P("row", "col", None)
    in_specs = (tile, tile, P("row", "col"), tile, P(), P(), P(), P(), P())
    out_specs = (tile, P(), P(), P(), P())
    return jax.shard_map(shards, mesh=mesh, in_specs=in_specs, out_specs=out_specs, check_vma=False)
```

time: 725 us -> 99.4 us (0.14)
  waiting for transfers between devices: 509 us -> 0 us
  blocking collectives: 126 us -> 0 us
  Pallas kernels: 0 us -> 89.3 us
  starting transfers between devices: 25.1 us -> 0 us
  matrix products: 16.2 us -> 0 us
  local copies, waits for them, and re-layouts: 24.4 us -> 8.33 us
  between operations: 14.4 us -> 0.67 us
  other arithmetic: 8.89 us -> 0.76 us
    psum x1 -> x0, waiting for transfers between devices: 458 us -> none  [shards(): lax.psum((part_win, part_wgate, part_wout, part_gain), ('row', 'col'))]
    psum x1 -> x0, blocking collectives: 110 us -> none  [shards(): lax.psum((part_win, part_wgate, part_wout, part_gain), ('row', 'col'))]
    pallas_call x0 -> x1, Pallas kernels: none -> 89.3 us  [shards(): pl.pallas_call(kernel, out_shape=(jax.ShapeDtypeStruct(tile, BF16), jax.S...]
    all_gather x1 -> x0, waiting for transfers between devices: 36.8 us -> none  [shards(): shard_rows = lax.all_gather(mix_slab, 'row', axis=1, tiled=True)]
    all_to_all x4 -> x0, starting transfers between devices: 25 us -> none  [the longest x1 13.1 us: shards(): lax.all_to_all(left_part.astype(jnp.bfloat16), 'col', split_axis=2, conca...]
    dot_general x11 -> x0, matrix products: 16.2 us -> none  [the longest x1 3.5 us: shards(): jnp.einsum('cki,cij->ckj', left_slab, shard_rows, preferred_element_type=...]
    all_to_all x1 -> x0, blocking collectives: 15.6 us -> none  [shards(): lax.all_to_all(mix_cf, 'col', split_axis=0, concat_axis=2, tiled=True)]
    all_to_all x4 -> x0, waiting for transfers between devices: 14.1 us -> none  [the longest x1 5.22 us: shards(): lax.all_to_all(left_part.astype(jnp.bfloat16), 'col', split_axis=2, conca...]
  transfers between devices with their start and end apart: 6 -> 0, of which waited for: 5 -> 0; matrix products, arithmetic and copies ran while one was open for 1% -> 0% of each run, Pallas kernels for 0% -> 0%
where the time goes in v1:
time: 99.4 us; the launch traced here: 99.1 us
  Pallas kernels  89.3 us (90%)
  local copies, waits for them, and re-layouts  8.33 us (8%)
    pallas_call x1, Pallas kernels, shards(): pl.pallas_call(kernel, out_shape=(jax.ShapeDtypeStruct(tile, BF16), jax.S...  89.3 us
    unnamed x19, local copies, waits for them, and re-layouts  7.32 us

profile of v1, /device:TPU:1, one launch (start us, length us, event | category | flops | bytes accessed | tf_op | source)
XLA Modules:
  0.0 99.1 jit_solution(4540871991613753575)
XLA Ops:
  0.6 0.0 copy-start.5
  0.6 0.0 copy-start.4
  0.7 0.7 convert_element_type.3
  1.3 0.1 dynamic_slice.7
  1.4 0.1 dynamic_slice.6
  1.5 0.8 reshape.44.rstd_ref
  2.3 0.1 broadcast_multiply_fusion
  2.3 0.0 copy-start.6
  2.3 0.1 mul.34.mask_ref
  2.4 0.0 copy-done.5
  2.4 0.0 copy-done.4
  2.4 0.6 copy-done.6
  3.0 0.0 copy-start
  3.0 0.9 copy-done
  3.9 0.0 copy-start.1
  3.9 0.9 copy-done.1
  4.8 0.0 copy-start.2
  4.8 0.9 copy-done.2
  5.7 0.0 copy-start.3
  5.7 0.9 copy-done.3
  6.6 89.3 %shard_map.128 = (bf16[16,32,128]{2,1,0:T(8,128)(2,1)S(1)}, f32[128,512]{1,0:T(8,128)S(1)}, f32[128,128]{1,0:T(8,128)S(1)}, f32[128,128]{1,0:T(8,128)S(1)}, f32[1,128]{1,0:T(1,128)S(1)}) custom-call(bf16[16,32,128]{2,1,0:T(8,128)(2,1)S(1)} %copy-done, bf16[16,32,128]{2,1,0:T(8,128)(2,1)S(1)} %copy-done.1, f32[1,512]{1,0:T(1,128)S(1)} %reshape.44.rstd_ref, ...), custom_call_target="tpu_custom_call" | custom-call | tf_op jit(solution)/shard_map/pallas_call | solution.py:351
  96.0 0.7 copy.19
  96.6 0.7 copy.20
  97.3 0.6 copy.21
  97.9 0.6 copy.22
  98.6 0.5 copy.23
Async XLA Ops:
  0.6 1.8 %copy-start.5 = (bf16[128,128]{1,0:T(8,128)(2,1)S(1)}, bf16[128,128]{1,0:T(8,128)(2,1)}, u32[]{:S(2)}) copy-start(bf16[128,128]{1,0:T(8,128)(2,1)} %wout_ref.1) | copy-start | bytes 98308
  0.6 1.8 %copy-start.4 = (bf16[128,128]{1,0:T(8,128)(2,1)S(1)}, bf16[128,128]{1,0:T(8,128)(2,1)}, u32[]{:S(2)}) copy-start(bf16[128,128]{1,0:T(8,128)(2,1)} %wgate_ref.1) | copy-start | bytes 98308
  2.3 0.7 copy-start.6
  3.0 0.9 copy-start
  3.9 0.9 copy-start.1
  4.8 0.9 copy-start.2
  5.7 0.9 copy-start.3

commit v2 on v1

v2 whole, which is shorter than its diff:
```python
import jax
import jax.numpy as jnp
from jax import lax
from jax.experimental import pallas as pl
from jax.experimental.pallas import tpu as pltpu
from jax.sharding import PartitionSpec as P

F32, BF16 = jnp.float32, jnp.bfloat16
MESH = pl.DeviceIdType.MESH

TOKENS = 512
WIDTH = 128
ROWS, COLS = 16, 32
PAIRS = ROWS * COLS
RING = 16
BANKS = 2
ACROSS = 16
PLANE = BANKS * ACROSS
SLOTS = WIDTH // PLANE
CHUNK = 128 // SLOTS


def mm(a, b, ca, cb):
    return lax.dot_general(a, b, (((ca,), (cb,)), ((), ())), preferred_element_type=F32)


def swap_chunks(parts):
    lane = lax.broadcasted_iota(jnp.int32, parts[0].shape, 1)
    low = lane < 64
    even = lax.rem(lane // CHUNK, 2) == 0
    a, b, c, d = parts
    a, c = jnp.where(low, a, pltpu.roll(c, 64, 1)), jnp.where(low, pltpu.roll(a, 64, 1), c)
    b, d = jnp.where(low, b, pltpu.roll(d, 64, 1)), jnp.where(low, pltpu.roll(b, 64, 1), d)
    a, b = jnp.where(even, a, pltpu.roll(b, 32, 1)), jnp.where(even, pltpu.roll(a, 96, 1), b)
    c, d = jnp.where(even, c, pltpu.roll(d, 32, 1)), jnp.where(even, pltpu.roll(c, 96, 1), d)
    return a, b, c, d


def to_tiles(values, work):
    parts = []
    for slot in range(SLOTS):
        block = values[slot * PLANE : (slot + 1) * PLANE]
        parts.append(jnp.concatenate([block[:, g * 128 : (g + 1) * 128] for g in range(4)], axis=0))
    for low, part in enumerate(swap_chunks(parts)):
        for g in range(4):
            work[pl.ds(4 * g + low, PLANE, stride=ROWS), :] = part[g * PLANE : (g + 1) * PLANE]
    return work[...].astype(BF16).reshape(PLANE, ROWS, 128)


def from_tiles(tiles, work):
    work[...] = tiles.astype(F32).reshape(PLANE * ROWS, 128)
    parts = []
    for low in range(4):
        parts.append(
            jnp.concatenate(
                [work[pl.ds(4 * g + low, PLANE, stride=ROWS), :] for g in range(4)], axis=0
            )
        )
    out = []
    for part in swap_chunks(parts):
        out.append(
            jnp.concatenate([part[g * PLANE : (g + 1) * PLANE] for g in range(4)], axis=1)
        )
    return jnp.concatenate(out, axis=0)


def gather_slab(tiles):
    tiles = tiles.astype(F32).reshape(BANKS, 4, 4, ROWS, 128)
    parts = [tiles[:, :, q].reshape(BANKS * 4 * ROWS, 128) for q in range(4)]
    out = []
    for part in swap_chunks(parts):
        part = part.reshape(BANKS, 4, ROWS, 128)
        out.append(
            jnp.concatenate([part[:, g].reshape(BANKS * ROWS, 128) for g in range(4)], axis=1)
        )
    return jnp.concatenate(out, axis=0)


def scatter_slab(slab):
    parts = []
    for slot in range(SLOTS):
        block = slab[slot * BANKS * ROWS : (slot + 1) * BANKS * ROWS]
        block = [
            block[:, g * 128 : (g + 1) * 128].reshape(BANKS, 1, ROWS, 128) for g in range(4)
        ]
        parts.append(jnp.concatenate(block, axis=1).reshape(BANKS * 4 * ROWS, 128))
    out = [
        part.reshape(BANKS, 4, 1, ROWS, 128) for part in swap_chunks(parts)
    ]
    return jnp.concatenate(out, axis=2).reshape(PLANE, ROWS, 128).astype(BF16)


def kernel(
    pair_hbm, hat_hbm, rstd_hbm, grad_hbm, mask_hbm, win_hbm, wgate_hbm, wout_hbm, gain_hbm,
    dpair_hbm, dwin_hbm, dsmall_hbm, dgain_hbm,
    pair_ref, hat_ref, rstd_ref, grad_ref, mask_ref, win_ref, wgate_ref, wout_ref, gain_ref,
    dpair_ref, dwin_ref, dsmall_ref, dgain_ref, work, mix_out, mix_in, lr_out, lr_in, factor_out, factor_in, back_out, back_in,
    held, right_diag, left_cols, left_sums, right_sums, factors, slab_factors, slab_proj, proj,
    pairs_all, small_out, small_in, small_half, small_ring, small_mine, small_all,
    win_half, win_ring, win_mine, win_all,
    load_sems, save_sems, ring_send, ring_recv, send_sems, recv_sems, x_send, x_recv,
):
    row, col = lax.axis_index("row"), lax.axis_index("col")
    bank, z = row // RING, lax.rem(row, RING)
    me = bank * ACROSS + col
    core = lax.rem(col, 2)
    at_x, at_y = lax.rem(col // 2, 4), bank * 2 + col // 8

    def plane_id(peer):
        return ((peer // ACROSS) * RING + z, lax.rem(peer, ACROSS))

    def ring_id(place):
        return (bank * RING + place, col)

    barrier = pltpu.get_barrier_semaphore()

    @pl.loop(1, PLANE)
    def _(t):
        pl.semaphore_signal(
            barrier, inc=1, device_id=plane_id(lax.rem(me + t, PLANE)), device_id_type=MESH
        )

    for t in (1, RING - 1):
        pl.semaphore_signal(
            barrier, inc=1, device_id=ring_id(lax.rem(z + t, RING)), device_id_type=MESH
        )

    loads = [
        pltpu.make_async_copy(source, target, load_sems.at[k])
        for k, (source, target) in enumerate(
            [
                (pair_hbm, pair_ref), (wgate_hbm, wgate_ref), (grad_hbm, grad_ref),
                (wout_hbm, wout_ref), (hat_hbm, hat_ref), (gain_hbm, gain_ref),
                (rstd_hbm, rstd_ref), (win_hbm, win_ref), (mask_hbm, mask_ref),
            ]
        )
    ]
    for load in loads:
        load.start()

    saves = [
        pltpu.make_async_copy(source, target, save_sems.at[k])
        for k, (source, target) in enumerate(
            [
                (dpair_ref, dpair_hbm), (dwin_ref, dwin_hbm),
                (dsmall_ref, dsmall_hbm), (dgain_ref, dgain_hbm),
            ]
        )
    ]
    received, sent = [], []

    def plane_send(source, target, k):
        received.append((target, PLANE, k))
        sent.append((target, PLANE, k))

        @pl.loop(1, PLANE)
        def _(t):
            peer = lax.rem(me + t, PLANE)
            pltpu.make_async_remote_copy(
                src_ref=source(peer), dst_ref=target.at[me],
                send_sem=send_sems.at[k], recv_sem=recv_sems.at[k],
                device_id=plane_id(peer), device_id_type=MESH,
            ).start()

    def ring_copy(source, target, offset, k):
        return pltpu.make_async_remote_copy(
            src_ref=source, dst_ref=target.at[z],
            send_sem=send_sems.at[k], recv_sem=recv_sems.at[k],
            device_id=ring_id(lax.rem(z + offset, RING)), device_id_type=MESH,
        )

    def ring_share(source, target, k, farthest=True):
        received.append((target, RING, k))
        sent.append((target, RING, k))

        @pl.loop(1, RING - 1)
        def _(t):
            ring_copy(source, target, t + t // (RING // 2), k).start()

        if farthest:
            ring_copy(source, target, RING // 2, k).start()

    def wait_bytes(ref, sem):
        pltpu.make_async_copy(ref, ref, sem).wait()

    def wait_many(target, count, k):
        received.remove((target, count, k))
        wait_bytes(target.at[pl.ds(0, count - 1)], recv_sems.at[k])

    hops, arrivals = [], []

    def drain():
        for target, count, k in received:
            wait_bytes(target.at[pl.ds(0, count - 1)], recv_sems.at[k])
        for target, count, k in sent:
            wait_bytes(target.at[pl.ds(0, count - 1)], send_sems.at[k])
        for key in arrivals:
            hop(*key).wait_recv()
        for key in hops:
            hop(*key).wait_send()
        for key in incoming:
            piece(*key).wait_recv()
        for key in outgoing:
            piece(*key).wait_send()

    def start_hop(way, s, part):
        hops.append((way, s, part))
        arrivals.append((way, s, part))
        hop(way, s, part).start()

    def await_hop(way, s, part):
        arrivals.remove((way, s, part))
        hop(way, s, part).wait_recv()

    def hop(way, s, part):
        step = 1 if way == 0 else RING - 1
        block = lax.rem(z + (RING - 1) * step * (s - 1), RING)
        return pltpu.make_async_remote_copy(
            src_ref=held.at[block, part], dst_ref=held.at[block, part],
            send_sem=ring_send.at[way, s - 1, part], recv_sem=ring_recv.at[way, s - 1, part],
            device_id=ring_id(lax.rem(z + step, RING)), device_id_type=MESH,
        )

    outgoing, incoming = [], []

    def piece(kind, dy, dx):
        ty, tx = lax.rem(at_y + dy, 4), lax.rem(at_x + dx, 4)
        rows = pl.ds(0, ROWS)
        to_y, to_x, to_core = at_y, at_x, core
        if kind == "core":
            to_core, k = 1 - core, 24 + 4 * dy + dx
        if kind[0] == "y":
            way = 1 if kind[1] == "+" else 3
            to_y = lax.rem(at_y + way, 4)
            if dy:
                rows = pl.ds(0 if way == 1 else ROWS // 2, ROWS // 2)
            k = (0 if way == 1 else 1) + (2 if dy else 0)
        if kind[0] == "x":
            way = 1 if kind[1] == "+" else 3
            to_x = lax.rem(at_x + way, 4)
            if dx:
                rows = pl.ds(0 if way == 1 else ROWS // 2, ROWS // 2)
            k = 4 + dy * 4 + (0 if way == 1 else 1) + (2 if dx else 0)
        place = pairs_all.at[ty // 2, rows, lax.rem(ty, 2) * 8 + tx * 2 + core]
        return pltpu.make_async_remote_copy(
            src_ref=place, dst_ref=place, send_sem=x_send.at[k], recv_sem=x_recv.at[k],
            device_id=((to_y // 2) * RING + z, lax.rem(to_y, 2) * 8 + to_x * 2 + to_core),
            device_id_type=MESH,
        )

    def pass_on(kind, dy, dx):
        outgoing.append((kind, dy, dx))
        incoming.append((kind, dy, dx))
        piece(kind, dy, dx).start()

    def take(kind, dy, dx):
        incoming.remove((kind, dy, dx))
        piece(kind, dy, dx).wait_recv()

    def relay(stage):
        if stage == 0:
            pairs_all[bank, :, col] = pair_ref[...]
            for way in "+-":
                pass_on("y" + way, 0, 0)
                pass_on("x" + way, 0, 0)
            pass_on("core", 0, 0)
        if stage == 1:
            take("y+", 0, 0)
            pass_on("y+", 3, 0)
            take("y-", 0, 0)
            pass_on("y-", 1, 0)
            for dy in (3, 1):
                for way in "+-":
                    pass_on("x" + way, dy, 0)
                pass_on("core", dy, 0)
            take("x+", 0, 0)
            pass_on("x+", 0, 3)
            take("x-", 0, 0)
            pass_on("x-", 0, 1)
            pass_on("core", 0, 3)
            pass_on("core", 0, 1)
        if stage == 2:
            take("y+", 3, 0)
            take("y-", 1, 0)
            for way in "+-":
                pass_on("x" + way, 2, 0)
            pass_on("core", 2, 0)
            for dy in (3, 1):
                take("x+", dy, 0)
                pass_on("x+", dy, 3)
                take("x-", dy, 0)
                pass_on("x-", dy, 1)
                pass_on("core", dy, 3)
                pass_on("core", dy, 1)
            take("x+", 0, 3)
            take("x-", 0, 1)
            pass_on("core", 0, 2)
        if stage == 3:
            take("x+", 2, 0)
            pass_on("x+", 2, 3)
            take("x-", 2, 0)
            pass_on("x-", 2, 1)
            pass_on("core", 2, 3)
            pass_on("core", 2, 1)
            for dy in (3, 1):
                take("x+", dy, 3)
                take("x-", dy, 1)
                pass_on("core", dy, 2)
        if stage == 4:
            take("x+", 2, 3)
            take("x-", 2, 1)
            pass_on("core", 2, 2)
        if stage == 5:
            for dy in range(4):
                for dx in range(4):
                    take("core", dy, dx)

    def column(values):
        return jnp.sum(jnp.where(diagonal, values, 0.0), axis=1, keepdims=True)

    diagonal = lax.broadcasted_iota(jnp.int32, (WIDTH, WIDTH), 0) == lax.broadcasted_iota(
        jnp.int32, (WIDTH, WIDTH), 1
    )
    for load in loads[:3]:
        load.wait()
    x = pair_ref[...].reshape(PAIRS, WIDTH)
    gate = jax.nn.sigmoid(mm(wgate_ref[...], x, 0, 1))
    grad = grad_ref[...].reshape(PAIRS, WIDTH).astype(F32).T
    gated = (grad * gate).astype(BF16)
    for load in loads[3:7]:
        load.wait()
    scaled_grad = mm(wout_ref[...], gated, 1, 0)
    hat = hat_ref[...].reshape(PAIRS, WIDTH).astype(F32).T
    gain = column(gain_ref[...])
    spread = jnp.concatenate([rstd_ref[...]] * ROWS, axis=1)
    own_row = lax.broadcasted_iota(jnp.int32, spread.shape, 1) // COLS
    own_row = own_row == lax.broadcasted_iota(jnp.int32, spread.shape, 0)
    rstd = jnp.sum(jnp.where(own_row, spread, 0.0), axis=0, keepdims=True)
    h = scaled_grad * gain
    mean_h = jnp.mean(h, axis=0, keepdims=True)
    mean_hx = jnp.mean(h * hat, axis=0, keepdims=True)
    mix = rstd * (h - mean_h - hat * mean_hx)
    mix_out[...] = to_tiles(mix, work)
    mix_in[me] = mix_out[me]
    for load in loads[7:]:
        load.wait()
    pl.semaphore_wait(barrier, PLANE + 1)
    plane_send(lambda peer: mix_out.at[peer], mix_in, 0)

    token = lax.broadcasted_iota(jnp.int32, (TOKENS, PAIRS), 0)
    pair = lax.broadcasted_iota(jnp.int32, (TOKENS, PAIRS), 1)
    mask = jnp.broadcast_to(mask_ref[...].astype(F32), (8, TOKENS)).astype(BF16)
    mask_row = mm(mask, (token == row * ROWS + pair // COLS).astype(BF16), 1, 0)
    mask_col = mm(mask, (token == col * COLS + lax.rem(pair, COLS)).astype(BF16), 1, 0)
    pair_mask = (mask_row * mask_col)[:1]
    projected = mm(win_ref[...], x, 0, 1)
    value_a, logit_a = projected[:WIDTH], projected[WIDTH : 2 * WIDTH]
    value_b, logit_b = projected[2 * WIDTH : 3 * WIDTH], projected[3 * WIDTH :]
    sigma_a, sigma_b = jax.nn.sigmoid(logit_a), jax.nn.sigmoid(logit_b)
    masked_a, masked_b = pair_mask * sigma_a, pair_mask * sigma_b
    lr_out[:, :ROWS] = to_tiles(masked_a * value_a, work)
    lr_out[:, ROWS:] = to_tiles(masked_b * value_b, work)
    lr_in[me] = lr_out[me]
    plane_send(lambda peer: lr_out.at[peer], lr_in, 1)
    factors[0] = masked_a
    factors[1] = masked_a * value_a * (1.0 - sigma_a)
    factors[2] = masked_b
    factors[3] = masked_b * value_b * (1.0 - sigma_b)

    wait_many(mix_in, PLANE, 0)
    slab = gather_slab(mix_in[...]).astype(BF16)
    for slot in range(SLOTS):
        held[z, slot // 2, :, (slot % 2) * TOKENS : (slot % 2 + 1) * TOKENS] = slab[
            slot * BANKS * ROWS : (slot + 1) * BANKS * ROWS
        ]
    for part in range(2):
        for way in range(2):
            start_hop(way, 1, part)
    relay(0)

    wait_many(lr_in, PLANE, 1)
    left_cols[...] = gather_slab(lr_in[:, :ROWS]).T.astype(BF16)
    right = gather_slab(lr_in[:, ROWS:]).astype(BF16)
    right_diag[...] = jnp.zeros_like(right_diag)
    for slot in range(SLOTS):
        rows = slice(slot * BANKS * ROWS, (slot + 1) * BANKS * ROWS)
        right_diag[slot // 2, rows, (slot % 2) * TOKENS : (slot % 2 + 1) * TOKENS] = right[rows]
    right_sums[...] = jnp.zeros_like(right_sums)

    def contract(part, blocks):
        mixes = jnp.concatenate([held[block, part] for block in blocks], axis=0)
        places = [
            pl.ds(pl.multiple_of(b * (TOKENS // BANKS) + block * ROWS, ROWS), ROWS)
            for block in blocks
            for b in range(BANKS)
        ]
        sums = mm(mixes, right_diag[part], 1, 1)
        for n, place in enumerate(places):
            values = sums[n * ROWS : (n + 1) * ROWS]
            if part:
                values = values + left_sums[place]
            left_sums[place] = values
        lefts = jnp.concatenate([left_cols[place] for place in places], axis=0)
        for c in range(2):
            rows = slice((2 * part + c) * BANKS * ROWS, (2 * part + c + 1) * BANKS * ROWS)
            right_sums[rows] += mm(
                lefts[:, rows], mixes[:, c * TOKENS : (c + 1) * TOKENS], 0, 0
            )

    def ring_step(s, last):
        for part in range(2):
            for way in range(2):
                await_hop(way, s, part)
                if not last or way == part:
                    start_hop(way, s + 1, part)
            contract(part, [lax.rem(z + RING - s, RING), lax.rem(z + s, RING)])

    contract(0, [z])
    contract(1, [z])
    ring_step(1, False)

    for n in range(4):
        factor_out[:, n * ROWS : (n + 1) * ROWS] = to_tiles(factors[n], work)
    factor_in[me] = factor_out[me]
    plane_send(lambda peer: factor_out.at[peer], factor_in, 2)
    ring_step(2, False)

    scaled = (hat * gain).astype(BF16)
    output = mm(wout_ref[...], scaled, 0, 0)
    gate_grad = (grad * output * gate * (1.0 - gate)).astype(BF16)
    proj[4 * WIDTH :] = gate_grad
    small_out[: PLANE // 2, :8] = mm(x, gate_grad, 0, 1).reshape(PLANE // 2, 8, WIDTH)
    small_out[PLANE // 2 :, :8] = mm(scaled, gated, 1, 1).reshape(PLANE // 2, 8, WIDTH)
    part_gain = jnp.sum(scaled_grad * hat, axis=1, keepdims=True)
    part_gain = jnp.sum(jnp.where(diagonal, part_gain, 0.0), axis=0, keepdims=True)
    small_out[:, 8:] = jnp.broadcast_to(part_gain[None], (PLANE, 8, WIDTH))
    small_in[me] = small_out[me]
    plane_send(lambda peer: small_out.at[peer], small_in, 3)
    ring_step(3, False)
    relay(1)
    ring_step(4, False)

    wait_many(factor_in, PLANE, 2)
    for n in range(4):
        slab_factors[n] = gather_slab(factor_in[:, n * ROWS : (n + 1) * ROWS]).astype(BF16)
    ring_step(5, False)
    relay(2)
    wait_many(small_in, PLANE, 3)
    small_half[...] = jnp.sum(small_in[...], axis=0).astype(BF16)
    small_ring[z] = small_half[...]
    ring_step(6, False)
    relay(3)
    ring_step(7, True)
    ring_share(small_half, small_ring, 4, False)
    relay(4)
    for part in range(2):
        await_hop(part, RING // 2, part)
        contract(part, [lax.rem(z + RING // 2, RING)])
    ring_copy(small_half, small_ring, RING // 2, 4).start()

    left_grad = left_sums[...].T
    for n in range(2):
        values = left_grad if n == 0 else right_sums[...]
        values = values.astype(BF16).astype(F32)
        for m in range(2):
            terms = values * slab_factors[2 * n + m].astype(F32)
            for g in range(4):
                slab_proj[g, (2 * n + m) * WIDTH : (2 * n + m + 1) * WIDTH] = terms[
                    :, g * 128 : (g + 1) * 128
                ]
    relay(5)
    total = jnp.zeros((4 * SLOTS, WIDTH), F32)
    for k in range(BANKS * ROWS):
        terms = jnp.concatenate(
            [slab_proj[g, pl.ds(k, 4 * SLOTS, stride=BANKS * ROWS), :] for g in range(4)], axis=1
        )
        pairs = pairs_all[k // ROWS, k % ROWS].reshape(TOKENS, WIDTH)
        total = total + mm(terms.astype(BF16), pairs, 1, 0)
    win_half[...] = total.astype(BF16)
    win_ring[z] = win_half[...]
    ring_share(win_half, win_ring, 5)

    back_out[:, :ROWS] = scatter_slab(left_grad)
    back_out[:, ROWS:] = scatter_slab(right_sums[...])
    back_in[me] = back_out[me]
    plane_send(lambda peer: back_out.at[peer], back_in, 6)

    def ring_total(ring):
        return jnp.sum(ring[...].astype(F32), axis=0) * (1.0 / TOKENS)

    wait_many(small_ring, RING, 4)
    small_mine[...] = ring_total(small_ring)
    dgain_ref[...] = small_mine[8:9]
    saves[3].start()
    small_all[me] = small_mine[:8]
    plane_send(lambda peer: small_mine.at[pl.ds(0, 8)], small_all, 7)

    wait_many(win_ring, RING, 5)
    win_mine[...] = ring_total(win_ring)
    win_all[me] = win_mine[...]
    plane_send(lambda peer: win_mine, win_all, 8)

    wait_many(back_in, PLANE, 6)
    grad_left = from_tiles(back_in[:, :ROWS], work)
    proj[:WIDTH] = (grad_left * factors[0]).astype(BF16)
    proj[WIDTH : 2 * WIDTH] = (grad_left * factors[1]).astype(BF16)
    grad_right = from_tiles(back_in[:, ROWS:], work)
    proj[2 * WIDTH : 3 * WIDTH] = (grad_right * factors[2]).astype(BF16)
    proj[3 * WIDTH : 4 * WIDTH] = (grad_right * factors[3]).astype(BF16)
    weights = jnp.concatenate([win_ref[...], wgate_ref[...]], axis=1)
    d_pair = mm(weights, proj[...], 1, 0)
    dpair_ref[...] = d_pair.T.astype(BF16).reshape(ROWS, COLS, WIDTH)
    saves[0].start()

    wait_many(small_all, PLANE, 7)
    dsmall_ref[...] = small_all[...].reshape(2 * WIDTH, WIDTH)
    saves[2].start()
    wait_many(win_all, PLANE, 8)
    work[...] = win_all[...].reshape(4 * WIDTH, WIDTH)
    dwin_ref[...] = jnp.concatenate(
        [work[pl.ds(n, PLANE, stride=4 * SLOTS), :] for n in range(4 * SLOTS)], axis=0
    ).T
    saves[1].start()
    drain()
    for save in saves:
        save.wait()


def finish(dpair, dwin, dsmall, dgain, dpair_out, dwin_out, dwgate_out, dwout_out, dgain_out, *rest):
    held, loads, saves = rest[:4], rest[4], rest[5]
    sources = [dpair, dwin, dsmall, dgain]
    first = [
        pltpu.make_async_copy(source, target, loads.at[k])
        for k, (source, target) in enumerate(zip(sources, held))
    ]
    last = [
        pltpu.make_async_copy(source, target, saves.at[k])
        for k, (source, target) in enumerate(
            [
                (held[0], dpair_out),
                (held[1], dwin_out),
                (held[2].at[pl.ds(0, WIDTH)], dwgate_out),
                (held[2].at[pl.ds(WIDTH, WIDTH)], dwout_out),
                (held[3], dgain_out),
            ]
        )
    ]
    for copy in first:
        copy.start()
    for k, copies in enumerate([last[:1], last[1:2], last[2:4], last[4:]]):
        first[k].wait()
        for copy in copies:
            copy.start()
    for copy in last:
        copy.wait()


def shards(pair_norm, out_hat, out_rstd, grad_out, token_mask, w_in, w_gate, w_out, ln_gain):
    tile = (ROWS, COLS, WIDTH)
    square = (WIDTH, WIDTH)
    hbm = pl.BlockSpec(memory_space=pltpu.HBM)
    shape = jax.ShapeDtypeStruct
    tiles = lambda rows, dtype: pltpu.VMEM((PLANE, rows, WIDTH), dtype)
    results = pl.pallas_call(
        kernel,
        out_shape=(
            shape(tile, BF16),
            shape((WIDTH, 4 * WIDTH), F32),
            shape((2 * WIDTH, WIDTH), F32),
            shape((1, WIDTH), F32),
        ),
        in_specs=[hbm] * 9,
        out_specs=[hbm] * 4,
        scratch_shapes=[
            pltpu.VMEM(tile, BF16),
            pltpu.VMEM(tile, BF16),
            pltpu.VMEM((ROWS, COLS), F32),
            pltpu.VMEM(tile, BF16),
            pltpu.VMEM((1, TOKENS), jnp.int32),
            pltpu.VMEM((WIDTH, 4 * WIDTH), BF16),
            pltpu.VMEM(square, BF16),
            pltpu.VMEM(square, BF16),
            pltpu.VMEM((1, WIDTH), F32),
            pltpu.VMEM(tile, BF16),
            pltpu.VMEM((WIDTH, 4 * WIDTH), F32),
            pltpu.VMEM((2 * WIDTH, WIDTH), F32),
            pltpu.VMEM((1, WIDTH), F32),
            pltpu.VMEM((PAIRS, WIDTH), F32),
            *[tiles(ROWS, BF16)] * 2,
            *[tiles(2 * ROWS, BF16)] * 2,
            *[tiles(4 * ROWS, BF16)] * 2,
            *[tiles(2 * ROWS, BF16)] * 2,
            pltpu.VMEM((RING, 2, BANKS * ROWS, 2 * TOKENS), BF16),
            pltpu.VMEM((2, WIDTH, 2 * TOKENS), BF16),
            pltpu.VMEM((TOKENS, WIDTH), BF16),
            pltpu.VMEM((TOKENS, WIDTH), F32),
            pltpu.VMEM((WIDTH, TOKENS), F32),
            pltpu.VMEM((4, WIDTH, PAIRS), F32),
            pltpu.VMEM((4, WIDTH, TOKENS), BF16),
            pltpu.VMEM((4, 4 * WIDTH, 128), F32),
            pltpu.VMEM((5 * WIDTH, PAIRS), BF16),
            pltpu.VMEM((BANKS, ROWS, ACROSS, COLS, WIDTH), BF16),
            tiles(ROWS, F32),
            tiles(ROWS, F32),
            pltpu.VMEM((ROWS, WIDTH), BF16),
            pltpu.VMEM((RING, ROWS, WIDTH), BF16),
            pltpu.VMEM((ROWS, WIDTH), F32),
            tiles(8, F32),
            pltpu.VMEM((ROWS, WIDTH), BF16),
            pltpu.VMEM((RING, ROWS, WIDTH), BF16),
            pltpu.VMEM((ROWS, WIDTH), F32),
            tiles(ROWS, F32),
            pltpu.SemaphoreType.DMA((9,)),
            pltpu.SemaphoreType.DMA((4,)),
            pltpu.SemaphoreType.DMA((2, RING // 2, 2)),
            pltpu.SemaphoreType.DMA((2, RING // 2, 2)),
            pltpu.SemaphoreType.DMA((9,)),
            pltpu.SemaphoreType.DMA((9,)),
            pltpu.SemaphoreType.DMA((40,)),
            pltpu.SemaphoreType.DMA((40,)),
        ],
        compiler_params=pltpu.CompilerParams(
            collective_id=0, has_side_effects=True, vmem_limit_bytes=62 * 1024 * 1024
        ),
    )(
        pair_norm, out_hat, out_rstd, grad_out, token_mask.reshape(1, TOKENS),
        w_in, w_gate, w_out, ln_gain.reshape(1, WIDTH),
    )
    d_pair, d_win, d_wgate, d_wout, d_gain = pl.pallas_call(
        finish,
        out_shape=(
            shape(tile, BF16),
            shape((WIDTH, 4 * WIDTH), F32),
            shape(square, F32),
            shape(square, F32),
            shape((1, WIDTH), F32),
        ),
        in_specs=[hbm] * 4,
        out_specs=[hbm] * 5,
        scratch_shapes=[
            pltpu.VMEM(tile, BF16),
            pltpu.VMEM((WIDTH, 4 * WIDTH), F32),
            pltpu.VMEM((2 * WIDTH, WIDTH), F32),
            pltpu.VMEM((1, WIDTH), F32),
            pltpu.SemaphoreType.DMA((4,)),
            pltpu.SemaphoreType.DMA((5,)),
        ],
        compiler_params=pltpu.CompilerParams(vmem_limit_bytes=62 * 1024 * 1024),
    )(*results)
    return d_pair, d_win, d_wgate, d_wout, d_gain.reshape(WIDTH)


def solution(mesh):
    tile = P("row", "col", None)
    in_specs = (tile, tile, P("row", "col"), tile, P(), P(), P(), P(), P())
    out_specs = (tile, P(), P(), P(), P())
    return jax.shard_map(shards, mesh=mesh, in_specs=in_specs, out_specs=out_specs, check_vma=False)
```

time: 99.4 us -> 75.6 us (0.76)
  Pallas kernels: 89.3 us -> 74.8 us
  local copies, waits for them, and re-layouts: 8.33 us -> 0 us
    pallas_call x1 -> x2, Pallas kernels: 89.3 us -> 74.8 us  [the longest x1 72.9 us: shards(): pl.pallas_call(kernel, out_shape=(shape(tile, BF16), shape((WIDTH, 4 * WI...]
    unnamed x19 -> x0, local copies, waits for them, and re-layouts: 7.32 us -> none
where the time goes in v2:
time: 75.6 us; the launch traced here: 75.4 us
  Pallas kernels  74.8 us (99%)
    pallas_call x1, Pallas kernels, shards(): pl.pallas_call(kernel, out_shape=(shape(tile, BF16), shape((WIDTH, 4 * WI...  72.9 us
    pallas_call x1, Pallas kernels, shards(): pl.pallas_call(finish, out_shape=(shape(tile, BF16), shape((WIDTH, 4 * WI...  1.84 us

profile of v2, /device:TPU:1, one launch (start us, length us, event | category | flops | bytes accessed | tf_op | source)
XLA Modules:
  0.0 75.4 jit_solution(7497660236491869666)
XLA Ops:
  0.6 72.9 %shard_map.128 = (bf16[16,32,128]{2,1,0:T(8,128)(2,1)}, f32[128,512]{1,0:T(8,128)}, f32[256,128]{1,0:T(8,128)}, f32[1,128]{1,0:T(1,128)}) custom-call(bf16[16,32,128]{2,1,0:T(8,128)(2,1)} %pair_hbm.1, bf16[16,32,128]{2,1,0:T(8,128)(2,1)} %hat_hbm.1, f32[16,32]{1,0:T(8,128)} %rstd_hbm.1, bf16[16,32,128]{2,1,0:T(8,128)(2,1)} %grad_hbm.1, s32[1,512]{1,0:T(1,128)} %bitcast.3, ...), custom_call_target="tpu_custom_call" | custom-call | tf_op jit(solution)/shard_map/pallas_call | solution.py:564
  73.6 1.8 %shard_map.129 = (bf16[16,32,128]{2,1,0:T(8,128)(2,1)}, f32[128,512]{1,0:T(8,128)}, f32[128,128]{1,0:T(8,128)}, f32[128,128]{1,0:T(8,128)}, f32[1,128]{1,0:T(1,128)}) custom-call(bf16[16,32,128]{2,1,0:T(8,128)(2,1)} %get-tuple-element.14.dpair, f32[128,512]{1,0:T(8,128)} %get-tuple-element.15.dwin, f32[256,128]{1,0:T(8,128)} %get-tuple-element.16.dsmall, ...), custom_call_target="tpu_custom_call" | custom-call | tf_op jit(solution)/shard_map/pallas_call | solution.py:629

commit v3 on v2

--- a/solution.py
+++ b/solution.py
@@ -18,6 +18,7 @@
 PLANE = BANKS * ACROSS
 SLOTS = WIDTH // PLANE
 CHUNK = 128 // SLOTS
+FAR_FIRST = (2, 3, 1, 0)
 
 
 def mm(a, b, ca, cb):
@@ -112,12 +113,29 @@
     def ring_id(place):
         return (bank * RING + place, col)
 
+    def far_first(t):
+        across, along, other = t // 8, lax.rem(t // 2, 4), 1 - lax.rem(t, 2)
+        dy, dx = (3 - n + (2 * n - 1) * (1 - n // 2) for n in (across, along))
+        return (
+            lax.rem(at_y + dy, 4) * 8
+            + lax.rem(at_x + dx, 4) * 2
+            + lax.rem(core + other, 2)
+        )
+
+    plane_y = [lax.rem(at_y + n, 4) for n in range(4)]
+    plane_row = [(y // 2) * RING + z for y in plane_y]
+    plane_col = [lax.rem(y, 2) * 8 for y in plane_y]
+    plane_x = [
+        [lax.rem(at_x + n, 4) * 2 + lax.rem(core + other, 2) for other in range(2)]
+        for n in range(4)
+    ]
+
     barrier = pltpu.get_barrier_semaphore()
 
-    @pl.loop(1, PLANE)
+    @pl.loop(0, PLANE - 1)
     def _(t):
         pl.semaphore_signal(
-            barrier, inc=1, device_id=plane_id(lax.rem(me + t, PLANE)), device_id_type=MESH
+            barrier, inc=1, device_id=plane_id(far_first(t)), device_id_type=MESH
         )
 
     for t in (1, RING - 1):
@@ -153,14 +171,16 @@
         received.append((target, PLANE, k))
         sent.append((target, PLANE, k))
 
-        @pl.loop(1, PLANE)
-        def _(t):
-            peer = lax.rem(me + t, PLANE)
-            pltpu.make_async_remote_copy(
-                src_ref=source(peer), dst_ref=target.at[me],
-                send_sem=send_sems.at[k], recv_sem=recv_sems.at[k],
-                device_id=plane_id(peer), device_id_type=MESH,
-            ).start()
+        for across, along in ((a, b) for a in FAR_FIRST for b in FAR_FIRST):
+            for other in (1, 0):
+                if across or along or other:
+                    peer = plane_y[across] * 8 + plane_x[along][other]
+                    pltpu.make_async_remote_copy(
+                        src_ref=source(peer), dst_ref=target.at[me],
+                        send_sem=send_sems.at[k], recv_sem=recv_sems.at[k],
+                        device_id=(plane_row[across], plane_col[across] + plane_x[along][other]),
+                        device_id_type=MESH,
+                    ).start()
 
     def ring_copy(source, target, offset, k):
         return pltpu.make_async_remote_copy(
@@ -173,12 +193,10 @@
         received.append((target, RING, k))
         sent.append((target, RING, k))
 
-        @pl.loop(1, RING - 1)
+        @pl.loop(0 if farthest else 1, RING - 1)
         def _(t):
-            ring_copy(source, target, t + t // (RING // 2), k).start()
-
-        if farthest:
-            ring_copy(source, target, RING // 2, k).start()
+            offset = RING // 2 + ((t + 1) // 2) * (2 * lax.rem(t + 1, 2) - 1)
+            ring_copy(source, target, offset, k).start()
 
     def wait_bytes(ref, sem):
         pltpu.make_async_copy(ref, ref, sem).wait()
@@ -203,21 +221,21 @@
         for key in outgoing:
             piece(*key).wait_send()
 
-    def start_hop(way, s, part):
-        hops.append((way, s, part))
-        arrivals.append((way, s, part))
-        hop(way, s, part).start()
-
-    def await_hop(way, s, part):
-        arrivals.remove((way, s, part))
-        hop(way, s, part).wait_recv()
-
-    def hop(way, s, part):
+    def start_hop(way, s, slot):
+        hops.append((way, s, slot))
+        arrivals.append((way, s, slot))
+        hop(way, s, slot).start()
+
+    def await_hop(way, s, slot):
+        arrivals.remove((way, s, slot))
+        hop(way, s, slot).wait_recv()
+
+    def hop(way, s, slot):
         step = 1 if way == 0 else RING - 1
         block = lax.rem(z + (RING - 1) * step * (s - 1), RING)
         return pltpu.make_async_remote_copy(
-            src_ref=held.at[block, part], dst_ref=held.at[block, part],
-            send_sem=ring_send.at[way, s - 1, part], recv_sem=ring_recv.at[way, s - 1, part],
+            src_ref=held.at[block, slot], dst_ref=held.at[block, slot],
+            send_sem=ring_send.at[way, s - 1, slot], recv_sem=ring_recv.at[way, s - 1, slot],
             device_id=ring_id(lax.rem(z + step, RING)), device_id_type=MESH,
         )
 
@@ -333,7 +351,7 @@
     hat = hat_ref[...].reshape(PAIRS, WIDTH).astype(F32).T
     gain = column(gain_ref[...])
     spread = jnp.concatenate([rstd_ref[...]] * ROWS, axis=1)
-    own_row = lax.broadcasted_iota(jnp.int32, spread.shape, 1) // COLS
+    own_row = lax.broadcasted_iota(jnp.int32, (1, PAIRS), 1) // COLS
     own_row = own_row == lax.broadcasted_iota(jnp.int32, spread.shape, 0)
     rstd = jnp.sum(jnp.where(own_row, spread, 0.0), axis=0, keepdims=True)
     h = scaled_grad * gain
@@ -348,10 +366,11 @@
     plane_send(lambda peer: mix_out.at[peer], mix_in, 0)
 
     token = lax.broadcasted_iota(jnp.int32, (TOKENS, PAIRS), 0)
-    pair = lax.broadcasted_iota(jnp.int32, (TOKENS, PAIRS), 1)
+    pair = lax.broadcasted_iota(jnp.int32, (1, PAIRS), 1)
     mask = jnp.broadcast_to(mask_ref[...].astype(F32), (8, TOKENS)).astype(BF16)
-    mask_row = mm(mask, (token == row * ROWS + pair // COLS).astype(BF16), 1, 0)
-    mask_col = mm(mask, (token == col * COLS + lax.rem(pair, COLS)).astype(BF16), 1, 0)
+    one_hot = lambda place: jnp.where(token == place, 1.0, 0.0).astype(BF16)
+    mask_row = mm(mask, one_hot(row * ROWS + pair // COLS), 1, 0)
+    mask_col = mm(mask, one_hot(col * COLS + lax.rem(pair, COLS)), 1, 0)
     pair_mask = (mask_row * mask_col)[:1]
     projected = mm(win_ref[...], x, 0, 1)
     value_a, logit_a = projected[:WIDTH], projected[WIDTH : 2 * WIDTH]
@@ -370,13 +389,10 @@
     wait_many(mix_in, PLANE, 0)
     slab = gather_slab(mix_in[...]).astype(BF16)
     for slot in range(SLOTS):
-        held[z, slot // 2, :, (slot % 2) * TOKENS : (slot % 2 + 1) * TOKENS] = slab[
-            slot * BANKS * ROWS : (slot + 1) * BANKS * ROWS
-        ]
-    for part in range(2):
+        held[z, slot] = slab[slot * BANKS * ROWS : (slot + 1) * BANKS * ROWS]
         for way in range(2):
-            start_hop(way, 1, part)
-    relay(0)
+            start_hop(way, 1, slot)
+
 
     wait_many(lr_in, PLANE, 1)
     left_cols[...] = gather_slab(lr_in[:, :ROWS]).T.astype(BF16)
@@ -384,39 +400,38 @@
     right_diag[...] = jnp.zeros_like(right_diag)
     for slot in range(SLOTS):
         rows = slice(slot * BANKS * ROWS, (slot + 1) * BANKS * ROWS)
-        right_diag[slot // 2, rows, (slot % 2) * TOKENS : (slot % 2 + 1) * TOKENS] = right[rows]
+        right_diag[rows, slot * TOKENS : (slot + 1) * TOKENS] = right[rows]
     right_sums[...] = jnp.zeros_like(right_sums)
 
-    def contract(part, blocks):
-        mixes = jnp.concatenate([held[block, part] for block in blocks], axis=0)
+    def contract(blocks):
+        mixes = [
+            jnp.concatenate([held[block, slot] for block in blocks], axis=0)
+            for slot in range(SLOTS)
+        ]
         places = [
             pl.ds(pl.multiple_of(b * (TOKENS // BANKS) + block * ROWS, ROWS), ROWS)
             for block in blocks
             for b in range(BANKS)
         ]
-        sums = mm(mixes, right_diag[part], 1, 1)
+        sums = mm(jnp.concatenate(mixes, axis=1), right_diag[...], 1, 1)
         for n, place in enumerate(places):
-            values = sums[n * ROWS : (n + 1) * ROWS]
-            if part:
-                values = values + left_sums[place]
-            left_sums[place] = values
-        lefts = jnp.concatenate([left_cols[place] for place in places], axis=0)
-        for c in range(2):
-            rows = slice((2 * part + c) * BANKS * ROWS, (2 * part + c + 1) * BANKS * ROWS)
-            right_sums[rows] += mm(
-                lefts[:, rows], mixes[:, c * TOKENS : (c + 1) * TOKENS], 0, 0
-            )
+            left_sums[place] = sums[n * ROWS : (n + 1) * ROWS]
+        lefts = jnp.concatenate([left_cols[place] for place in places], axis=0).astype(F32)
+        lefts = lefts.T.astype(BF16)
+        for slot in range(SLOTS):
+            rows = slice(slot * BANKS * ROWS, (slot + 1) * BANKS * ROWS)
+            right_sums[rows] += mm(lefts[rows], mixes[slot], 1, 0)
 
     def ring_step(s, last):
-        for part in range(2):
+        for slot in range(SLOTS):
             for way in range(2):
-                await_hop(way, s, part)
-                if not last or way == part:
-                    start_hop(way, s + 1, part)
-            contract(part, [lax.rem(z + RING - s, RING), lax.rem(z + s, RING)])
-
-    contract(0, [z])
-    contract(1, [z])
+                await_hop(way, s, slot)
+                if not last or way == slot // 2:
+                    start_hop(way, s + 1, slot)
+        contract([lax.rem(z + RING - s, RING), lax.rem(z + s, RING)])
+
+    contract([z])
+    relay(0)
     ring_step(1, False)
 
     for n in range(4):
@@ -437,26 +452,26 @@
     small_in[me] = small_out[me]
     plane_send(lambda peer: small_out.at[peer], small_in, 3)
     ring_step(3, False)
+    ring_step(4, False)
     relay(1)
-    ring_step(4, False)
 
     wait_many(factor_in, PLANE, 2)
     for n in range(4):
         slab_factors[n] = gather_slab(factor_in[:, n * ROWS : (n + 1) * ROWS]).astype(BF16)
     ring_step(5, False)
-    relay(2)
     wait_many(small_in, PLANE, 3)
     small_half[...] = jnp.sum(small_in[...], axis=0).astype(BF16)
     small_ring[z] = small_half[...]
     ring_step(6, False)
-    relay(3)
+    relay(2)
     ring_step(7, True)
     ring_share(small_half, small_ring, 4, False)
+    relay(3)
+    for slot in range(SLOTS):
+        await_hop(slot // 2, RING // 2, slot)
+    ring_copy(small_half, small_ring, RING // 2, 4).start()
     relay(4)
-    for part in range(2):
-        await_hop(part, RING // 2, part)
-        contract(part, [lax.rem(z + RING // 2, RING)])
-    ring_copy(small_half, small_ring, RING // 2, 4).start()
+    contract([lax.rem(z + RING // 2, RING)])
 
     left_grad = left_sums[...].T
     for n in range(2):
@@ -496,7 +511,7 @@
     plane_send(lambda peer: small_mine.at[pl.ds(0, 8)], small_all, 7)
 
     wait_many(win_ring, RING, 5)
-    win_mine[...] = ring_total(win_ring)
+    win_mine[...] = ring_total(win_ring).astype(BF16)
     win_all[me] = win_mine[...]
     plane_send(lambda peer: win_mine, win_all, 8)
 
@@ -516,7 +531,7 @@
     dsmall_ref[...] = small_all[...].reshape(2 * WIDTH, WIDTH)
     saves[2].start()
     wait_many(win_all, PLANE, 8)
-    work[...] = win_all[...].reshape(4 * WIDTH, WIDTH)
+    work[...] = win_all[...].astype(F32).reshape(4 * WIDTH, WIDTH)
     dwin_ref[...] = jnp.concatenate(
         [work[pl.ds(n, PLANE, stride=4 * SLOTS), :] for n in range(4 * SLOTS)], axis=0
     ).T
@@ -590,8 +605,8 @@
             *[tiles(2 * ROWS, BF16)] * 2,
             *[tiles(4 * ROWS, BF16)] * 2,
             *[tiles(2 * ROWS, BF16)] * 2,
-            pltpu.VMEM((RING, 2, BANKS * ROWS, 2 * TOKENS), BF16),
-            pltpu.VMEM((2, WIDTH, 2 * TOKENS), BF16),
+            pltpu.VMEM((RING, SLOTS, BANKS * ROWS, TOKENS), BF16),
+            pltpu.VMEM((WIDTH, SLOTS * TOKENS), BF16),
             pltpu.VMEM((TOKENS, WIDTH), BF16),
             pltpu.VMEM((TOKENS, WIDTH), F32),
             pltpu.VMEM((WIDTH, TOKENS), F32),
@@ -608,12 +623,12 @@
             tiles(8, F32),
             pltpu.VMEM((ROWS, WIDTH), BF16),
             pltpu.VMEM((RING, ROWS, WIDTH), BF16),
-            pltpu.VMEM((ROWS, WIDTH), F32),
-            tiles(ROWS, F32),
+            pltpu.VMEM((ROWS, WIDTH), BF16),
+            tiles(ROWS, BF16),
             pltpu.SemaphoreType.DMA((9,)),
             pltpu.SemaphoreType.DMA((4,)),
-            pltpu.SemaphoreType.DMA((2, RING // 2, 2)),
-            pltpu.SemaphoreType.DMA((2, RING // 2, 2)),
+            pltpu.SemaphoreType.DMA((2, RING // 2, SLOTS)),
+            pltpu.SemaphoreType.DMA((2, RING // 2, SLOTS)),
             pltpu.SemaphoreType.DMA((9,)),
             pltpu.SemaphoreType.DMA((9,)),
             pltpu.SemaphoreType.DMA((40,)),

time: 75.6 us -> 73.6 us (0.974)
  Pallas kernels: 74.8 us -> 72.8 us
    pallas_call x1, Pallas kernels: 72.9 us -> 70.9 us  [shards(): pl.pallas_call(kernel, out_shape=(shape(tile, BF16), shape((WIDTH, 4 * WI...]
where the time goes in v3:
time: 73.6 us; the launch traced here: 73.4 us
  Pallas kernels  72.8 us (99%)
    pallas_call x1, Pallas kernels, shards(): pl.pallas_call(kernel, out_shape=(shape(tile, BF16), shape((WIDTH, 4 * WI...  70.9 us
    pallas_call x1, Pallas kernels, shards(): pl.pallas_call(finish, out_shape=(shape(tile, BF16), shape((WIDTH, 4 * WI...  1.84 us

profile of v3, /device:TPU:1, one launch (start us, length us, event | category | flops | bytes accessed | tf_op | source)
XLA Modules:
  0.0 73.4 jit_solution(18139360668555150278)
XLA Ops:
  0.6 70.9 %shard_map.128 = (bf16[16,32,128]{2,1,0:T(8,128)(2,1)}, f32[128,512]{1,0:T(8,128)}, f32[256,128]{1,0:T(8,128)}, f32[1,128]{1,0:T(1,128)}) custom-call(bf16[16,32,128]{2,1,0:T(8,128)(2,1)} %pair_hbm.1, bf16[16,32,128]{2,1,0:T(8,128)(2,1)} %hat_hbm.1, f32[16,32]{1,0:T(8,128)} %rstd_hbm.1, bf16[16,32,128]{2,1,0:T(8,128)(2,1)} %grad_hbm.1, s32[1,512]{1,0:T(1,128)} %bitcast.3, ...), custom_call_target="tpu_custom_call" | custom-call | tf_op jit(solution)/shard_map/pallas_call | solution.py:579
  71.6 1.8 %shard_map.129 = (bf16[16,32,128]{2,1,0:T(8,128)(2,1)}, f32[128,512]{1,0:T(8,128)}, f32[128,128]{1,0:T(8,128)}, f32[128,128]{1,0:T(8,128)}, f32[1,128]{1,0:T(1,128)}) custom-call(bf16[16,32,128]{2,1,0:T(8,128)(2,1)} %get-tuple-element.14.dpair, f32[128,512]{1,0:T(8,128)} %get-tuple-element.15.dwin, f32[256,128]{1,0:T(8,128)} %get-tuple-element.16.dsmall, ...), custom_call_target="tpu_custom_call" | custom-call | tf_op jit(solution)/shard_map/pallas_call | solution.py:644

commit v4 on v3

--- a/solution.py
+++ b/solution.py
@@ -165,10 +165,9 @@
             ]
         )
     ]
-    received, sent = [], []
+    sent = []
 
     def plane_send(source, target, k):
-        received.append((target, PLANE, k))
         sent.append((target, PLANE, k))
 
         for across, along in ((a, b) for a in FAR_FIRST for b in FAR_FIRST):
@@ -190,7 +189,6 @@
         )
 
     def ring_share(source, target, k, farthest=True):
-        received.append((target, RING, k))
         sent.append((target, RING, k))
 
         @pl.loop(0 if farthest else 1, RING - 1)
@@ -202,135 +200,104 @@
         pltpu.make_async_copy(ref, ref, sem).wait()
 
     def wait_many(target, count, k):
-        received.remove((target, count, k))
         wait_bytes(target.at[pl.ds(0, count - 1)], recv_sems.at[k])
 
-    hops, arrivals = [], []
-
-    def drain():
-        for target, count, k in received:
-            wait_bytes(target.at[pl.ds(0, count - 1)], recv_sems.at[k])
+    def start_hop(way, s, slot):
+        hop(way, s, slot).start()
+
+    def await_hop(way, s, slot):
+        hop(way, s, slot).wait_recv()
+
+    def settle():
         for target, count, k in sent:
             wait_bytes(target.at[pl.ds(0, count - 1)], send_sems.at[k])
-        for key in arrivals:
-            hop(*key).wait_recv()
-        for key in hops:
-            hop(*key).wait_send()
-        for key in incoming:
-            piece(*key).wait_recv()
-        for key in outgoing:
-            piece(*key).wait_send()
-
-    def start_hop(way, s, slot):
-        hops.append((way, s, slot))
-        arrivals.append((way, s, slot))
-        hop(way, s, slot).start()
-
-    def await_hop(way, s, slot):
-        arrivals.remove((way, s, slot))
-        hop(way, s, slot).wait_recv()
+        sent.clear()
 
     def hop(way, s, slot):
         step = 1 if way == 0 else RING - 1
         block = lax.rem(z + (RING - 1) * step * (s - 1), RING)
         return pltpu.make_async_remote_copy(
             src_ref=held.at[block, slot], dst_ref=held.at[block, slot],
-            send_sem=ring_send.at[way, s - 1, slot], recv_sem=ring_recv.at[way, s - 1, slot],
+            send_sem=ring_send.at[way], recv_sem=ring_recv.at[way, s - 1, slot],
             device_id=ring_id(lax.rem(z + step, RING)), device_id_type=MESH,
         )
 
-    outgoing, incoming = [], []
-
-    def piece(kind, dy, dx):
+    def piece(kind, first, second, turn):
+        dy, dx = (second, first) if turn else (first, second)
         ty, tx = lax.rem(at_y + dy, 4), lax.rem(at_x + dx, 4)
-        rows = pl.ds(0, ROWS)
-        to_y, to_x, to_core = at_y, at_x, core
-        if kind == "core":
-            to_core, k = 1 - core, 24 + 4 * dy + dx
-        if kind[0] == "y":
+        rows, k = pl.ds(0, ROWS), 40 + 4 * dy + dx
+        to_y, to_x, to_core = at_y, at_x, 1 - core
+        if kind != "core":
             way = 1 if kind[1] == "+" else 3
-            to_y = lax.rem(at_y + way, 4)
-            if dy:
-                rows = pl.ds(0 if way == 1 else ROWS // 2, ROWS // 2)
-            k = (0 if way == 1 else 1) + (2 if dy else 0)
-        if kind[0] == "x":
-            way = 1 if kind[1] == "+" else 3
-            to_x = lax.rem(at_x + way, 4)
-            if dx:
-                rows = pl.ds(0 if way == 1 else ROWS // 2, ROWS // 2)
-            k = 4 + dy * 4 + (0 if way == 1 else 1) + (2 if dx else 0)
+            far = first if kind[0] == "f" else second
+            low, count = turn * ROWS // 2, ROWS // 2
+            if far:
+                low, count = low + (way // 2) * ROWS // 4, ROWS // 4
+            rows = pl.ds(low, count)
+            if (kind[0] == "f") == (turn == 0):
+                to_y = lax.rem(at_y + way, 4)
+            else:
+                to_x = lax.rem(at_x + way, 4)
+            to_core = core
+            k = way // 2 + (2 if far else 0) + 20 * turn
+            if kind[0] == "s":
+                k += 4 + 4 * first
         place = pairs_all.at[ty // 2, rows, lax.rem(ty, 2) * 8 + tx * 2 + core]
         return pltpu.make_async_remote_copy(
-            src_ref=place, dst_ref=place, send_sem=x_send.at[k], recv_sem=x_recv.at[k],
+            src_ref=place, dst_ref=place,
+            send_sem=x_send.at[int(kind == "core")], recv_sem=x_recv.at[k],
             device_id=((to_y // 2) * RING + z, lax.rem(to_y, 2) * 8 + to_x * 2 + to_core),
             device_id_type=MESH,
         )
 
-    def pass_on(kind, dy, dx):
-        outgoing.append((kind, dy, dx))
-        incoming.append((kind, dy, dx))
-        piece(kind, dy, dx).start()
-
-    def take(kind, dy, dx):
-        incoming.remove((kind, dy, dx))
-        piece(kind, dy, dx).wait_recv()
+    def pass_on(kind, first, second, turn=0):
+        piece(kind, first, second, turn).start()
+
+    def take(kind, first, second, turn=0):
+        piece(kind, first, second, turn).wait_recv()
 
     def relay(stage):
         if stage == 0:
             pairs_all[bank, :, col] = pair_ref[...]
-            for way in "+-":
-                pass_on("y" + way, 0, 0)
-                pass_on("x" + way, 0, 0)
-            pass_on("core", 0, 0)
-        if stage == 1:
-            take("y+", 0, 0)
-            pass_on("y+", 3, 0)
-            take("y-", 0, 0)
-            pass_on("y-", 1, 0)
-            for dy in (3, 1):
+        for turn in range(2):
+            if stage == 0:
                 for way in "+-":
-                    pass_on("x" + way, dy, 0)
-                pass_on("core", dy, 0)
-            take("x+", 0, 0)
-            pass_on("x+", 0, 3)
-            take("x-", 0, 0)
-            pass_on("x-", 0, 1)
-            pass_on("core", 0, 3)
-            pass_on("core", 0, 1)
-        if stage == 2:
-            take("y+", 3, 0)
-            take("y-", 1, 0)
-            for way in "+-":
-                pass_on("x" + way, 2, 0)
-            pass_on("core", 2, 0)
-            for dy in (3, 1):
-                take("x+", dy, 0)
-                pass_on("x+", dy, 3)
-                take("x-", dy, 0)
-                pass_on("x-", dy, 1)
-                pass_on("core", dy, 3)
-                pass_on("core", dy, 1)
-            take("x+", 0, 3)
-            take("x-", 0, 1)
-            pass_on("core", 0, 2)
-        if stage == 3:
-            take("x+", 2, 0)
-            pass_on("x+", 2, 3)
-            take("x-", 2, 0)
-            pass_on("x-", 2, 1)
-            pass_on("core", 2, 3)
-            pass_on("core", 2, 1)
-            for dy in (3, 1):
-                take("x+", dy, 3)
-                take("x-", dy, 1)
-                pass_on("core", dy, 2)
-        if stage == 4:
-            take("x+", 2, 3)
-            take("x-", 2, 1)
-            pass_on("core", 2, 2)
-        if stage == 5:
-            for dy in range(4):
-                for dx in range(4):
+                    pass_on("f" + way, 0, 0, turn)
+                    pass_on("s" + way, 0, 0, turn)
+            if stage == 1:
+                for way, side in (("+", 3), ("-", 1)):
+                    take("f" + way, 0, 0, turn)
+                    pass_on("f" + way, side, 0, turn)
+                    for to in "+-":
+                        pass_on("s" + to, side, 0, turn)
+                    take("s" + way, 0, 0, turn)
+                    pass_on("s" + way, 0, side, turn)
+            if stage == 2:
+                take("f+", 3, 0, turn)
+                take("f-", 1, 0, turn)
+                for way in "+-":
+                    pass_on("s" + way, 2, 0, turn)
+                for first in (3, 1):
+                    for way, side in (("+", 3), ("-", 1)):
+                        take("s" + way, first, 0, turn)
+                        pass_on("s" + way, first, side, turn)
+                take("s+", 0, 3, turn)
+                take("s-", 0, 1, turn)
+            if stage == 3:
+                for way, side in (("+", 3), ("-", 1)):
+                    take("s" + way, 2, 0, turn)
+                    pass_on("s" + way, 2, side, turn)
+                for first in (3, 1):
+                    take("s+", first, 3, turn)
+                    take("s-", first, 1, turn)
+            if stage == 4:
+                take("s+", 2, 3, turn)
+                take("s-", 2, 1, turn)
+        for dy in range(4):
+            for dx in range(4):
+                if stage == min(dy, 4 - dy) + min(dx, 4 - dx):
+                    pass_on("core", dy, dx)
+                if stage in (5, 6) and (stage == 6) == (2 in (dy, dx)):
                     take("core", dy, dx)
 
     def column(values):
@@ -386,6 +353,18 @@
     factors[2] = masked_b
     factors[3] = masked_b * value_b * (1.0 - sigma_b)
 
+    scaled = (hat * gain).astype(BF16)
+    output = mm(wout_ref[...], scaled, 0, 0)
+    gate_grad = (grad * output * gate * (1.0 - gate)).astype(BF16)
+    proj[4 * WIDTH :] = gate_grad
+    squares = [mm(x, gate_grad, 0, 1), mm(scaled, gated, 1, 1)]
+    squares = jnp.concatenate(squares, axis=0).reshape(PLANE, 8, WIDTH)
+    part_gain = jnp.sum(scaled_grad * hat, axis=1, keepdims=True)
+    part_gain = jnp.sum(jnp.where(diagonal, part_gain, 0.0), axis=0, keepdims=True)
+    part_gain = jnp.broadcast_to(part_gain[None], (PLANE, 8, WIDTH))
+    small_out[...] = jnp.concatenate([squares, part_gain], axis=1).astype(BF16)
+    small_in[me] = small_out[me]
+
     wait_many(mix_in, PLANE, 0)
     slab = gather_slab(mix_in[...]).astype(BF16)
     for slot in range(SLOTS):
@@ -433,45 +412,37 @@
     contract([z])
     relay(0)
     ring_step(1, False)
-
-    for n in range(4):
-        factor_out[:, n * ROWS : (n + 1) * ROWS] = to_tiles(factors[n], work)
+    factor_out[:, 0 * ROWS : 1 * ROWS] = to_tiles(factors[0], work)
+    factor_out[:, 1 * ROWS : 2 * ROWS] = to_tiles(factors[1], work)
+    factor_out[:, 2 * ROWS : 3 * ROWS] = to_tiles(factors[2], work)
+    factor_out[:, 3 * ROWS : 4 * ROWS] = to_tiles(factors[3], work)
+    ring_step(2, False)
     factor_in[me] = factor_out[me]
     plane_send(lambda peer: factor_out.at[peer], factor_in, 2)
-    ring_step(2, False)
-
-    scaled = (hat * gain).astype(BF16)
-    output = mm(wout_ref[...], scaled, 0, 0)
-    gate_grad = (grad * output * gate * (1.0 - gate)).astype(BF16)
-    proj[4 * WIDTH :] = gate_grad
-    small_out[: PLANE // 2, :8] = mm(x, gate_grad, 0, 1).reshape(PLANE // 2, 8, WIDTH)
-    small_out[PLANE // 2 :, :8] = mm(scaled, gated, 1, 1).reshape(PLANE // 2, 8, WIDTH)
-    part_gain = jnp.sum(scaled_grad * hat, axis=1, keepdims=True)
-    part_gain = jnp.sum(jnp.where(diagonal, part_gain, 0.0), axis=0, keepdims=True)
-    small_out[:, 8:] = jnp.broadcast_to(part_gain[None], (PLANE, 8, WIDTH))
-    small_in[me] = small_out[me]
+    ring_step(3, False)
+    relay(1)
     plane_send(lambda peer: small_out.at[peer], small_in, 3)
-    ring_step(3, False)
     ring_step(4, False)
-    relay(1)
-
+    ring_step(5, False)
+    relay(2)
     wait_many(factor_in, PLANE, 2)
-    for n in range(4):
-        slab_factors[n] = gather_slab(factor_in[:, n * ROWS : (n + 1) * ROWS]).astype(BF16)
-    ring_step(5, False)
+    slab_factors[0] = gather_slab(factor_in[:, 0 * ROWS : 1 * ROWS]).astype(BF16)
+    slab_factors[1] = gather_slab(factor_in[:, 1 * ROWS : 2 * ROWS]).astype(BF16)
+    slab_factors[2] = gather_slab(factor_in[:, 2 * ROWS : 3 * ROWS]).astype(BF16)
+    slab_factors[3] = gather_slab(factor_in[:, 3 * ROWS : 4 * ROWS]).astype(BF16)
+    ring_step(6, False)
+    relay(3)
     wait_many(small_in, PLANE, 3)
-    small_half[...] = jnp.sum(small_in[...], axis=0).astype(BF16)
+    small_half[...] = jnp.sum(small_in[...].astype(F32), axis=0).astype(BF16)
     small_ring[z] = small_half[...]
-    ring_step(6, False)
-    relay(2)
     ring_step(7, True)
     ring_share(small_half, small_ring, 4, False)
-    relay(3)
+    relay(4)
     for slot in range(SLOTS):
         await_hop(slot // 2, RING // 2, slot)
     ring_copy(small_half, small_ring, RING // 2, 4).start()
-    relay(4)
     contract([lax.rem(z + RING // 2, RING)])
+    relay(5)
 
     left_grad = left_sums[...].T
     for n in range(2):
@@ -483,7 +454,7 @@
                 slab_proj[g, (2 * n + m) * WIDTH : (2 * n + m + 1) * WIDTH] = terms[
                     :, g * 128 : (g + 1) * 128
                 ]
-    relay(5)
+    relay(6)
     total = jnp.zeros((4 * SLOTS, WIDTH), F32)
     for k in range(BANKS * ROWS):
         terms = jnp.concatenate(
@@ -510,6 +481,11 @@
     small_all[me] = small_mine[:8]
     plane_send(lambda peer: small_mine.at[pl.ds(0, 8)], small_all, 7)
 
+    settle()
+    for way in range(2):
+        wait_bytes(held.at[pl.ds(0, RING - 1), pl.ds(0, 2)], ring_send.at[way])
+    wait_bytes(pairs_all.at[0, :, pl.ds(0, ACROSS - 1)], x_send.at[0])
+    wait_bytes(pairs_all.at[0], x_send.at[1])
     wait_many(win_ring, RING, 5)
     win_mine[...] = ring_total(win_ring).astype(BF16)
     win_all[me] = win_mine[...]
@@ -536,7 +512,7 @@
         [work[pl.ds(n, PLANE, stride=4 * SLOTS), :] for n in range(4 * SLOTS)], axis=0
     ).T
     saves[1].start()
-    drain()
+    settle()
     for save in saves:
         save.wait()
 
@@ -615,8 +591,8 @@
             pltpu.VMEM((4, 4 * WIDTH, 128), F32),
             pltpu.VMEM((5 * WIDTH, PAIRS), BF16),
             pltpu.VMEM((BANKS, ROWS, ACROSS, COLS, WIDTH), BF16),
-            tiles(ROWS, F32),
-            tiles(ROWS, F32),
+            tiles(ROWS, BF16),
+            tiles(ROWS, BF16),
             pltpu.VMEM((ROWS, WIDTH), BF16),
             pltpu.VMEM((RING, ROWS, WIDTH), BF16),
             pltpu.VMEM((ROWS, WIDTH), F32),
@@ -627,12 +603,12 @@
             tiles(ROWS, BF16),
             pltpu.SemaphoreType.DMA((9,)),
             pltpu.SemaphoreType.DMA((4,)),
-            pltpu.SemaphoreType.DMA((2, RING // 2, SLOTS)),
+            pltpu.SemaphoreType.DMA((2,)),
             pltpu.SemaphoreType.DMA((2, RING // 2, SLOTS)),
             pltpu.SemaphoreType.DMA((9,)),
             pltpu.SemaphoreType.DMA((9,)),
-            pltpu.SemaphoreType.DMA((40,)),
-            pltpu.SemaphoreType.DMA((40,)),
+            pltpu.SemaphoreType.DMA((2,)),
+            pltpu.SemaphoreType.DMA((56,)),
         ],
         compiler_params=pltpu.CompilerParams(
             collective_id=0, has_side_effects=True, vmem_limit_bytes=62 * 1024 * 1024

time: 73.6 us -> 71.7 us (0.974)
  Pallas kernels: 72.8 us -> 70.9 us
    pallas_call x1, Pallas kernels: 70.9 us -> 69 us  [shards(): pl.pallas_call(kernel, out_shape=(shape(tile, BF16), shape((WIDTH, 4 * WI...]
where the time goes in v4:
time: 71.7 us; the launch traced here: 71.5 us
  Pallas kernels  70.9 us (99%)
    pallas_call x1, Pallas kernels, shards(): pl.pallas_call(kernel, out_shape=(shape(tile, BF16), shape((WIDTH, 4 * WI...  69 us
    pallas_call x1, Pallas kernels, shards(): pl.pallas_call(finish, out_shape=(shape(tile, BF16), shape((WIDTH, 4 * WI...  1.84 us

profile of v4, /device:TPU:1, one launch (start us, length us, event | category | flops | bytes accessed | tf_op | source)
XLA Modules:
  0.0 71.5 jit_solution(4615257739334376069)
XLA Ops:
  0.6 69.0 %shard_map.128 = (bf16[16,32,128]{2,1,0:T(8,128)(2,1)}, f32[128,512]{1,0:T(8,128)}, f32[256,128]{1,0:T(8,128)}, f32[1,128]{1,0:T(1,128)}) custom-call(bf16[16,32,128]{2,1,0:T(8,128)(2,1)} %pair_hbm.1, bf16[16,32,128]{2,1,0:T(8,128)(2,1)} %hat_hbm.1, f32[16,32]{1,0:T(8,128)} %rstd_hbm.1, bf16[16,32,128]{2,1,0:T(8,128)(2,1)} %grad_hbm.1, s32[1,512]{1,0:T(1,128)} %bitcast.3, ...), custom_call_target="tpu_custom_call" | custom-call | tf_op jit(solution)/shard_map/pallas_call | solution.py:555
  69.7 1.8 %shard_map.129 = (bf16[16,32,128]{2,1,0:T(8,128)(2,1)}, f32[128,512]{1,0:T(8,128)}, f32[128,128]{1,0:T(8,128)}, f32[128,128]{1,0:T(8,128)}, f32[1,128]{1,0:T(1,128)}) custom-call(bf16[16,32,128]{2,1,0:T(8,128)(2,1)} %get-tuple-element.14.dpair, f32[128,512]{1,0:T(8,128)} %get-tuple-element.15.dwin, f32[256,128]{1,0:T(8,128)} %get-tuple-element.16.dsmall, ...), custom_call_target="tpu_custom_call" | custom-call | tf_op jit(solution)/shard_map/pallas_call | solution.py:620

commit v5 on v4

--- a/solution.py
+++ b/solution.py
@@ -438,11 +438,11 @@
     ring_step(7, True)
     ring_share(small_half, small_ring, 4, False)
     relay(4)
+    relay(5)
     for slot in range(SLOTS):
         await_hop(slot // 2, RING // 2, slot)
     ring_copy(small_half, small_ring, RING // 2, 4).start()
     contract([lax.rem(z + RING // 2, RING)])
-    relay(5)
 
     left_grad = left_sums[...].T
     for n in range(2):
@@ -484,8 +484,6 @@
     settle()
     for way in range(2):
         wait_bytes(held.at[pl.ds(0, RING - 1), pl.ds(0, 2)], ring_send.at[way])
-    wait_bytes(pairs_all.at[0, :, pl.ds(0, ACROSS - 1)], x_send.at[0])
-    wait_bytes(pairs_all.at[0], x_send.at[1])
     wait_many(win_ring, RING, 5)
     win_mine[...] = ring_total(win_ring).astype(BF16)
     win_all[me] = win_mine[...]
@@ -503,6 +501,8 @@
     dpair_ref[...] = d_pair.T.astype(BF16).reshape(ROWS, COLS, WIDTH)
     saves[0].start()
 
+    wait_bytes(pairs_all.at[0, :, pl.ds(0, ACROSS - 1)], x_send.at[0])
+    wait_bytes(pairs_all.at[0], x_send.at[1])
     wait_many(small_all, PLANE, 7)
     dsmall_ref[...] = small_all[...].reshape(2 * WIDTH, WIDTH)
     saves[2].start()

time: 71.7 us -> 71.6 us (level)
  no operation moved by 1% of the time
where the time goes in v5:
time: 71.6 us; the launch traced here: 71.5 us
  Pallas kernels  70.8 us (99%)
    pallas_call x1, Pallas kernels, shards(): pl.pallas_call(kernel, out_shape=(shape(tile, BF16), shape((WIDTH, 4 * WI...  69 us
    pallas_call x1, Pallas kernels, shards(): pl.pallas_call(finish, out_shape=(shape(tile, BF16), shape((WIDTH, 4 * WI...  1.84 us

profile of v5, /device:TPU:1, one launch (start us, length us, event | category | flops | bytes accessed | tf_op | source)
XLA Modules:
  0.0 71.5 jit_solution(15686512028259268917)
XLA Ops:
  0.6 69.0 %shard_map.128 = (bf16[16,32,128]{2,1,0:T(8,128)(2,1)}, f32[128,512]{1,0:T(8,128)}, f32[256,128]{1,0:T(8,128)}, f32[1,128]{1,0:T(1,128)}) custom-call(bf16[16,32,128]{2,1,0:T(8,128)(2,1)} %pair_hbm.1, bf16[16,32,128]{2,1,0:T(8,128)(2,1)} %hat_hbm.1, f32[16,32]{1,0:T(8,128)} %rstd_hbm.1, bf16[16,32,128]{2,1,0:T(8,128)(2,1)} %grad_hbm.1, s32[1,512]{1,0:T(1,128)} %bitcast.3, ...), custom_call_target="tpu_custom_call" | custom-call | tf_op jit(solution)/shard_map/pallas_call | solution.py:555
  69.6 1.8 %shard_map.129 = (bf16[16,32,128]{2,1,0:T(8,128)(2,1)}, f32[128,512]{1,0:T(8,128)}, f32[128,128]{1,0:T(8,128)}, f32[128,128]{1,0:T(8,128)}, f32[1,128]{1,0:T(1,128)}) custom-call(bf16[16,32,128]{2,1,0:T(8,128)(2,1)} %get-tuple-element.14.dpair, f32[128,512]{1,0:T(8,128)} %get-tuple-element.15.dwin, f32[256,128]{1,0:T(8,128)} %get-tuple-element.16.dsmall, ...), custom_call_target="tpu_custom_call" | custom-call | tf_op jit(solution)/shard_map/pallas_call | solution.py:620
